TPU v7x, 32 devices: a whole 2x2x4 slice. The times are simulated.
32 devices in a mesh: dp: 4 (over y, x), ctx: 8 (over z, core).
Axes of the slice: x: 2, y: 2, z: 4, core: 2. Of those that a mesh axis runs over, the one named last changes fastest.
Arguments:
- tokens: bfloat16 [8192, 576], P(('dp', 'ctx')), may hold values from -6 to 6
- segment_ids: int32 [8192], P(('dp', 'ctx')), may hold values from 0 to 2, as said below
- positions: int32 [8192], P(('dp', 'ctx')), may hold values from 0 to 6143, as said below
- norm_gains: bfloat16 [2, 576], P(None, 'ctx'), may hold values from 0.099609375 to 1.8984375
- w_query: bfloat16 [576, 576], P('ctx', 'dp'), may hold values from -0.25 to 0.25
- w_key: bfloat16 [576, 192], P('ctx', 'dp'), may hold values from -0.25 to 0.25
- w_value: bfloat16 [576, 192], P('ctx', 'dp'), may hold values from -0.25 to 0.25
- w_out: bfloat16 [576, 576], P('ctx', 'dp'), may hold values from -6 to 6
- w_gate: bfloat16 [576, 1536], P('ctx', 'dp'), may hold values from -0.25 to 0.25
- w_up: bfloat16 [576, 1536], P('ctx', 'dp'), may hold values from -0.25 to 0.25
- w_down: bfloat16 [1536, 576], P('ctx', 'dp'), may hold values from -0.15625 to 0.15625
- cotangent: bfloat16 [8192, 576], P(('dp', 'ctx')), may hold values from -6 to 6
Outputs:
- mixed: bfloat16 [8192, 576], P(('dp', 'ctx'))
- token_grad: float32 [8192, 576], P(('dp', 'ctx'))
- gain_grad: float32 [2, 576], P(None, 'ctx')
- query_grad: float32 [576, 576], P('ctx', 'dp')
- key_grad: float32 [576, 192], P('ctx', 'dp')
- value_grad: float32 [576, 192], P('ctx', 'dp')
- out_grad: float32 [576, 576], P('ctx', 'dp')
- gate_grad: float32 [576, 1536], P('ctx', 'dp')
- up_grad: float32 [576, 1536], P('ctx', 'dp')
- down_grad: float32 [1536, 576], P('ctx', 'dp')
Inputs may be any that keep to these rules, and one draw needn't show every extreme that they name: `segment_ids`: in each sequence of 2048 tokens the numbers never fall from token to token; document 1 begins within the first 256 tokens and ends within the last 256. `positions`: within a document the position rises by one from token to token; document 1 begins at position 0; the last token of each sequence has the largest position.
All inputs are finite; a program needn't handle non-finite values.
Results may differ from a plain program's by a relative error of at most 0.015.
Values may be sent and summed in bfloat16 or wider, within the bound.
A program may use at most 128 MiB of HBM per device.

v0:
```python
import jax
import jax.numpy as jnp
from jax import lax
from jax.sharding import PartitionSpec as P

HEADS = 9
KV_HEADS = 3
HEAD = 64


EPSILON = 1e-05
ROPE_BASE = 100000.0
MASKED = -1e30


def tables(positions):
    half_dim = HEAD // 2
    frequency = ROPE_BASE ** (-(2.0 / HEAD) * jnp.arange(half_dim, dtype=jnp.float32))
    angles = positions.astype(jnp.float32)[:, None] * frequency[None, :]
    return (jnp.cos(angles)[:, None, :], jnp.sin(angles)[:, None, :])


def rotate(values, cosine_table, sine_table):
    half_dim = HEAD // 2
    per_head = values.reshape(values.shape[0], -1, HEAD)
    leading = per_head[..., :half_dim]
    trailing = per_head[..., half_dim:]
    turned = jnp.concatenate(
        [
            leading * cosine_table - trailing * sine_table,
            trailing * cosine_table + leading * sine_table,
        ],
        axis=-1,
    )
    return turned.reshape(values.shape)


def norm_back(hidden, inverse, gain_row, upstream):
    normed = hidden * inverse
    weighted = gain_row * upstream
    gain_part = jnp.sum(upstream * normed, axis=0)
    input_part = inverse * (weighted - normed * jnp.mean(weighted * normed, axis=1, keepdims=True))
    return (input_part, gain_part)


def gather_weights(shards, gain_rows):
    widened = (
        lax.all_gather(shards[0], "dp", axis=1, tiled=True),
        lax.all_gather(shards[1], "dp", axis=1, tiled=True),
        lax.all_gather(shards[2], "dp", axis=1, tiled=True),
        lax.all_gather(shards[3], "dp", axis=1, tiled=True),
        lax.all_gather(shards[4], "dp", axis=1, tiled=True),
        lax.all_gather(shards[5], "dp", axis=1, tiled=True),
        lax.all_gather(shards[6], "dp", axis=1, tiled=True),
    )
    complete = (
        lax.all_gather(widened[0], "ctx", axis=0, tiled=True),
        lax.all_gather(widened[1], "ctx", axis=0, tiled=True),
        lax.all_gather(widened[2], "ctx", axis=0, tiled=True),
        lax.all_gather(widened[3], "ctx", axis=0, tiled=True),
        lax.all_gather(widened[4], "ctx", axis=0, tiled=True),
        lax.all_gather(widened[5], "ctx", axis=0, tiled=True),
        lax.all_gather(widened[6], "ctx", axis=0, tiled=True),
        lax.all_gather(gain_rows, "ctx", axis=1, tiled=True),
    )
    return (
        (complete[0], complete[1], complete[2], complete[3], complete[4], complete[5], complete[6]),
        complete[7],
    )


def gather_keys(key_values, segments_low):
    return (
        lax.all_gather(key_values, "ctx", axis=0, tiled=True),
        lax.all_gather(segments_low, "ctx", axis=0, tiled=True),
    )


def key_blocks(gathered, rows_here):
    key_values, key_segments = gathered
    length = key_values.shape[0]
    block_width = min(length, 4 * rows_here)
    block_count = length // block_width
    return (
        key_values.reshape(block_count, block_width, key_values.shape[1]),
        key_segments.reshape(block_count, block_width),
        jnp.arange(block_count, dtype=jnp.int32) * block_width,
    )


def block_scores(query_head_rows, block_args, query_segments, query_index, logit_scale):
    key_block, segment_block, block_start = block_args
    block_width = key_block.shape[0]
    key_width = KV_HEADS * HEAD
    key_head_rows = key_block[:, :key_width].reshape(block_width, KV_HEADS, HEAD)
    value_head_rows = key_block[:, key_width:].reshape(block_width, KV_HEADS, HEAD)
    key_index = block_start + jnp.arange(block_width, dtype=jnp.int32)
    keep_mask = (query_segments[:, None] == segment_block[None, :]) & (
        key_index[None, :] <= query_index[:, None]
    )
    raw_scores = (
        jnp.einsum(
            "xikj,uij->ikxu", query_head_rows, key_head_rows, preferred_element_type=jnp.float32
        )
        * logit_scale
    )
    return (raw_scores, keep_mask, key_head_rows, value_head_rows)


def attend_forward(query_head_rows, gathered, query_segments, query_index, logit_scale):
    rows_here = query_head_rows.shape[0]
    blocks = key_blocks(gathered, rows_here)

    def stat_step(carry, block_args):
        row_top, row_total = carry
        raw_scores, keep_mask, key_head_rows, value_head_rows = block_scores(
            query_head_rows, block_args, query_segments, query_index, logit_scale
        )
        masked = jnp.where(keep_mask, raw_scores, MASKED)
        new_top = jnp.maximum(row_top, jnp.max(masked, axis=-1))
        row_total = row_total * jnp.exp(row_top - new_top) + jnp.sum(
            jnp.where(keep_mask, jnp.exp(masked - new_top[..., None]), 0.0), axis=-1
        )
        return ((new_top, row_total), None)

    stat_shape = (KV_HEADS, HEADS // KV_HEADS, rows_here)
    start_carry = (jnp.full(stat_shape, MASKED, jnp.float32), jnp.zeros(stat_shape, jnp.float32))
    (row_top, row_total), unused = lax.scan(stat_step, start_carry, blocks)
    log_total = row_top + jnp.log(row_total)

    def out_step(accumulated, block_args):
        raw_scores, keep_mask, key_head_rows, value_head_rows = block_scores(
            query_head_rows, block_args, query_segments, query_index, logit_scale
        )
        softmax_reduced = jnp.where(
            keep_mask, jnp.exp(raw_scores - log_total[..., None]), 0.0
        ).astype(jnp.bfloat16)
        return (
            accumulated
            + jnp.einsum(
                "ejfy,yex->fejx",
                softmax_reduced,
                value_head_rows,
                preferred_element_type=jnp.float32,
            ),
            None,
        )

    attention_output, unused = lax.scan(
        out_step, jnp.zeros(query_head_rows.shape, jnp.float32), blocks
    )
    return (log_total, attention_output)


def attend_backward(
    query_head_rows,
    gathered,
    query_segments,
    query_index,
    logit_scale,
    log_total,
    attention_output,
    attention_output_grad,
):
    rows_here = query_head_rows.shape[0]
    blocks = key_blocks(gathered, rows_here)
    row_correction = jnp.einsum(
        "qxmv,qxmv->xmq", attention_output_grad.astype(jnp.float32), attention_output
    )

    def back_step(accumulated, block_args):
        raw_scores, keep_mask, key_head_rows, value_head_rows = block_scores(
            query_head_rows, block_args, query_segments, query_index, logit_scale
        )
        probability = jnp.where(keep_mask, jnp.exp(raw_scores - log_total[..., None]), 0.0)
        slopes = jnp.einsum(
            "xikj,uij->ikxu",
            attention_output_grad,
            value_head_rows,
            preferred_element_type=jnp.float32,
        )
        score_gradient = (probability * (slopes - row_correction[..., None])).astype(jnp.bfloat16)
        accumulated = accumulated + jnp.einsum(
            "ejfy,yex->fejx", score_gradient, key_head_rows, preferred_element_type=jnp.float32
        )
        key_part = jnp.einsum(
            "qjif,iqjn->fqn", score_gradient, query_head_rows, preferred_element_type=jnp.float32
        )
        value_part = jnp.einsum(
            "qjif,iqjn->fqn",
            probability.astype(jnp.bfloat16),
            attention_output_grad,
            preferred_element_type=jnp.float32,
        )
        block_width = key_head_rows.shape[0]
        return (
            accumulated,
            jnp.concatenate(
                [key_part.reshape(block_width, -1), value_part.reshape(block_width, -1)], axis=1
            ),
        )

    query_part, stacked = lax.scan(back_step, jnp.zeros(query_head_rows.shape, jnp.float32), blocks)
    return (query_part, stacked.reshape(-1, stacked.shape[-1]))


def body(
    tokens,
    segment_ids,
    positions,
    norm_gains,
    w_query,
    w_key,
    w_value,
    w_out,
    w_gate,
    w_up,
    w_down,
    cotangent,
):
    shards = (w_query, w_key, w_value, w_out, w_gate, w_up, w_down)
    weights, gain_rows = gather_weights(shards, norm_gains)
    repeat = HEADS // KV_HEADS
    key_width = KV_HEADS * HEAD
    logit_scale = HEAD ** (-0.5)
    rows_here = tokens.shape[0]
    query_index = lax.axis_index("ctx") * rows_here + jnp.arange(rows_here, dtype=jnp.int32)
    cosine_table, sine_table = tables(positions)
    hidden = tokens.astype(jnp.float32)
    gain_one = gain_rows[0].astype(jnp.float32)
    gain_two = gain_rows[1].astype(jnp.float32)
    inverse_one = lax.rsqrt(jnp.mean(hidden * hidden, axis=1, keepdims=True) + EPSILON)
    normed_one = (hidden * inverse_one * gain_one).astype(jnp.bfloat16)
    queries = rotate(
        jnp.dot(normed_one, weights[0], preferred_element_type=jnp.float32),
        cosine_table,
        sine_table,
    ).astype(jnp.bfloat16)
    key_proj = rotate(
        jnp.dot(normed_one, weights[1], preferred_element_type=jnp.float32),
        cosine_table,
        sine_table,
    ).astype(jnp.bfloat16)
    value_proj = jnp.dot(normed_one, weights[2], preferred_element_type=jnp.float32).astype(
        jnp.bfloat16
    )
    key_values = jnp.concatenate([key_proj, value_proj], axis=1)
    segments_low = segment_ids.astype(jnp.bfloat16)
    gathered = gather_keys(key_values, segments_low)
    query_head_rows = queries.reshape(rows_here, KV_HEADS, repeat, HEAD)
    log_total, attention_output = attend_forward(
        query_head_rows, gathered, segments_low, query_index, logit_scale
    )
    attended_low = attention_output.reshape(rows_here, HEADS * HEAD).astype(jnp.bfloat16)
    middle = hidden + jnp.dot(attended_low, weights[3], preferred_element_type=jnp.float32)
    inverse_two = lax.rsqrt(jnp.mean(middle * middle, axis=1, keepdims=True) + EPSILON)
    normed_two = (middle * inverse_two * gain_two).astype(jnp.bfloat16)
    gate_out = jnp.dot(normed_two, weights[4], preferred_element_type=jnp.float32)
    up_out = jnp.dot(normed_two, weights[5], preferred_element_type=jnp.float32)
    inner_act = (jax.nn.silu(gate_out) * up_out).astype(jnp.bfloat16)
    mixed_out = (
        middle + jnp.dot(inner_act, weights[6], preferred_element_type=jnp.float32)
    ).astype(jnp.bfloat16)
    weights, gain_rows = gather_weights(shards, norm_gains)
    gathered = gather_keys(key_values, segments_low)
    down_weight_grad = jnp.einsum(
        "tf,td->fd", inner_act, cotangent, preferred_element_type=jnp.float32
    )
    inner_grad = jnp.einsum("td,fd->tf", cotangent, weights[6], preferred_element_type=jnp.float32)
    sigmoid_gate = jax.nn.sigmoid(gate_out)
    silu_gate = gate_out * sigmoid_gate
    gate_grad_low = (
        inner_grad * up_out * sigmoid_gate * (1.0 + gate_out * (1.0 - sigmoid_gate))
    ).astype(jnp.bfloat16)
    up_grad_low = (inner_grad * silu_gate).astype(jnp.bfloat16)
    gate_weight_grad = jnp.einsum(
        "td,tf->df", normed_two, gate_grad_low, preferred_element_type=jnp.float32
    )
    up_weight_grad = jnp.einsum(
        "td,tf->df", normed_two, up_grad_low, preferred_element_type=jnp.float32
    )
    normed_two_grad = jnp.einsum(
        "tf,df->td", gate_grad_low, weights[4], preferred_element_type=jnp.float32
    )
    normed_two_grad = normed_two_grad + jnp.einsum(
        "tf,df->td", up_grad_low, weights[5], preferred_element_type=jnp.float32
    )
    middle_grad, gain_two_grad = norm_back(middle, inverse_two, gain_two, normed_two_grad)
    middle_grad = middle_grad + cotangent.astype(jnp.float32)
    branch_low = middle_grad.astype(jnp.bfloat16)
    out_weight_grad = jnp.einsum(
        "tc,td->cd", attended_low, branch_low, preferred_element_type=jnp.float32
    )
    attention_output_grad = jnp.einsum(
        "td,cd->tc", branch_low, weights[3], preferred_element_type=jnp.float32
    ).astype(jnp.bfloat16)
    query_part, key_value_part = attend_backward(
        query_head_rows,
        gathered,
        segments_low,
        query_index,
        logit_scale,
        log_total,
        attention_output,
        attention_output_grad.reshape(rows_here, KV_HEADS, repeat, HEAD),
    )
    own_grads = lax.psum_scatter(key_value_part, "ctx", scatter_dimension=0, tiled=True)
    query_low = rotate(
        query_part.reshape(rows_here, HEADS * HEAD) * logit_scale, cosine_table, -sine_table
    ).astype(jnp.bfloat16)
    key_low = rotate(own_grads[:, :key_width] * logit_scale, cosine_table, -sine_table).astype(
        jnp.bfloat16
    )
    value_low = own_grads[:, key_width:].astype(jnp.bfloat16)
    query_weight_grad = jnp.einsum(
        "td,tc->dc", normed_one, query_low, preferred_element_type=jnp.float32
    )
    key_weight_grad = jnp.einsum(
        "td,tc->dc", normed_one, key_low, preferred_element_type=jnp.float32
    )
    value_weight_grad = jnp.einsum(
        "td,tc->dc", normed_one, value_low, preferred_element_type=jnp.float32
    )
    normed_one_grad = jnp.einsum(
        "tc,dc->td", query_low, weights[0], preferred_element_type=jnp.float32
    )
    normed_one_grad = normed_one_grad + jnp.einsum(
        "tc,dc->td", key_low, weights[1], preferred_element_type=jnp.float32
    )
    normed_one_grad = normed_one_grad + jnp.einsum(
        "tc,dc->td", value_low, weights[2], preferred_element_type=jnp.float32
    )
    hidden_grad, gain_one_grad = norm_back(hidden, inverse_one, gain_one, normed_one_grad)
    token_grad = middle_grad + hidden_grad
    gain_terms = jnp.stack([gain_one_grad, gain_two_grad])
    reduced = (
        lax.psum_scatter(query_weight_grad, "ctx", scatter_dimension=0, tiled=True),
        lax.psum_scatter(key_weight_grad, "ctx", scatter_dimension=0, tiled=True),
        lax.psum_scatter(value_weight_grad, "ctx", scatter_dimension=0, tiled=True),
        lax.psum_scatter(out_weight_grad, "ctx", scatter_dimension=0, tiled=True),
        lax.psum_scatter(gate_weight_grad, "ctx", scatter_dimension=0, tiled=True),
        lax.psum_scatter(up_weight_grad, "ctx", scatter_dimension=0, tiled=True),
        lax.psum_scatter(down_weight_grad, "ctx", scatter_dimension=0, tiled=True),
        lax.psum_scatter(gain_terms, "ctx", scatter_dimension=1, tiled=True),
    )
    copies = jnp.tile(reduced[7], (1, lax.axis_size("dp")))
    owned_grads = (
        lax.psum_scatter(
            reduced[0].astype(jnp.bfloat16), "dp", scatter_dimension=1, tiled=True
        ).astype(jnp.float32),
        lax.psum_scatter(
            reduced[1].astype(jnp.bfloat16), "dp", scatter_dimension=1, tiled=True
        ).astype(jnp.float32),
        lax.psum_scatter(
            reduced[2].astype(jnp.bfloat16), "dp", scatter_dimension=1, tiled=True
        ).astype(jnp.float32),
        lax.psum_scatter(
            reduced[3].astype(jnp.bfloat16), "dp", scatter_dimension=1, tiled=True
        ).astype(jnp.float32),
        lax.psum_scatter(
            reduced[4].astype(jnp.bfloat16), "dp", scatter_dimension=1, tiled=True
        ).astype(jnp.float32),
        lax.psum_scatter(
            reduced[5].astype(jnp.bfloat16), "dp", scatter_dimension=1, tiled=True
        ).astype(jnp.float32),
        lax.psum_scatter(
            reduced[6].astype(jnp.bfloat16), "dp", scatter_dimension=1, tiled=True
        ).astype(jnp.float32),
        lax.psum_scatter(copies.astype(jnp.bfloat16), "dp", scatter_dimension=1, tiled=True).astype(
            jnp.float32
        ),
    )
    return (
        mixed_out,
        token_grad,
        owned_grads[7],
        owned_grads[0],
        owned_grads[1],
        owned_grads[2],
        owned_grads[3],
        owned_grads[4],
        owned_grads[5],
        owned_grads[6],
    )


def solution(mesh):
    placed = (
        P(("dp", "ctx"), None),
        P(("dp", "ctx")),
        P(("dp", "ctx")),
        P(None, "ctx"),
        P("ctx", "dp"),
        P("ctx", "dp"),
        P("ctx", "dp"),
        P("ctx", "dp"),
        P("ctx", "dp"),
        P("ctx", "dp"),
        P("ctx", "dp"),
        P(("dp", "ctx"), None),
    )
    return jax.shard_map(
        body,
        mesh=mesh,
        in_specs=placed,
        out_specs=(
            P(("dp", "ctx"), None),
            P(("dp", "ctx"), None),
            P(None, "ctx"),
            P("ctx", "dp"),
            P("ctx", "dp"),
            P("ctx", "dp"),
            P("ctx", "dp"),
            P("ctx", "dp"),
            P("ctx", "dp"),
            P("ctx", "dp"),
        ),
        check_vma=False,
    )
```

profile of v0, /device:TPU:0, one launch (start us, length us, event | category | flops | bytes accessed | tf_op | source)
XLA Modules:
  0.0 659.2 jit_solution(8316091352165824948)
XLA Ops:
  9.1 13.5 %all-gather = bf16[8,72,2]{1,2,0:T(2,128)(2,1)S(1)} all-gather(bf16[1,72,2]{1,2,0:T(2,128)(2,1)} %bitcast.285), channel_id=1, replica_groups=mesh['dp'=4,'ctx'=8] {'ctx'}, dimensions={0}, use_global_device_ids=true | all-gather | bytes 2592 | tf_op jit(solution)/shard_map/all_gather | solution.py:64
  22.7 8.4 %all_gather.68 = bf16[72,192]{0,1:T(8,128)(2,1)S(1)} all-gather(bf16[72,48]{0,1:T(8,128)(2,1)} %param.23), channel_id=1, replica_groups=mesh['dp'=4,'ctx'=8] {'dp'}, dimensions={1}, use_global_device_ids=true | all-gather | bytes 34560 | tf_op jit(solution)/shard_map/all_gather | solution.py:49
  31.2 8.1 %all_gather.70 = bf16[72,192]{0,1:T(8,128)(2,1)S(1)} all-gather(bf16[72,48]{0,1:T(8,128)(2,1)} %param.24), channel_id=1, replica_groups=mesh['dp'=4,'ctx'=8] {'dp'}, dimensions={1}, use_global_device_ids=true | all-gather | bytes 34560 | tf_op jit(solution)/shard_map/all_gather | solution.py:50
  39.4 14.3 %all_gather.71 = bf16[576,192]{1,0:T(8,128)(2,1)S(1)} all-gather(bf16[72,192]{1,0:T(8,128)(2,1)S(1)} %copy.121), channel_id=1, replica_groups=mesh['dp'=4,'ctx'=8] {'ctx'}, dimensions={0}, use_global_device_ids=true | all-gather | bytes 248832 | tf_op jit(solution)/shard_map/all_gather | solution.py:59
  53.7 14.3 %all_gather.69 = bf16[576,192]{1,0:T(8,128)(2,1)S(1)} all-gather(bf16[72,192]{1,0:T(8,128)(2,1)S(1)} %copy.120), channel_id=1, replica_groups=mesh['dp'=4,'ctx'=8] {'ctx'}, dimensions={0}, use_global_device_ids=true | all-gather | bytes 248832 | tf_op jit(solution)/shard_map/all_gather | solution.py:58
  68.0 1.5 convolution_convert_fusion.1
  69.5 1.4 fusion.66
  72.6 8.9 %all_gather.80 = bf16[72,1536]{1,0:T(8,128)(2,1)} all-gather(bf16[72,384]{1,0:T(8,128)(2,1)S(1)} %copy-done.36), channel_id=1, replica_groups=mesh['dp'=4,'ctx'=8] {'dp'}, dimensions={1}, use_global_device_ids=true | all-gather | bytes 276480 | tf_op jit(solution)/shard_map/all_gather | solution.py:53
  81.6 9.9 %all_gather.78 = bf16[72,1536]{1,0:T(8,128)(2,1)} all-gather(bf16[72,384]{1,0:T(8,128)(2,1)S(1)} %copy-done.37), channel_id=1, replica_groups=mesh['dp'=4,'ctx'=8] {'dp'}, dimensions={1}, use_global_device_ids=true | all-gather | bytes 276480 | tf_op jit(solution)/shard_map/all_gather | solution.py:52
  91.6 8.1 %all_gather.82 = bf16[192,576]{0,1:T(8,128)(2,1)S(1)} all-gather(bf16[192,144]{0,1:T(8,128)(2,1)S(1)} %copy-done.35), channel_id=1, replica_groups=mesh['dp'=4,'ctx'=8] {'dp'}, dimensions={1}, use_global_device_ids=true | all-gather | bytes 276480 | tf_op jit(solution)/shard_map/all_gather | solution.py:54
  100.7 8.9 %all-gather.1 = bf16[8,1,256]{2,1,0:T(2,128)(2,1)S(1)} all-gather(bf16[1,1,256]{2,1,0:T(2,128)(2,1)S(1)} %reshape.215), channel_id=1, replica_groups=mesh['dp'=4,'ctx'=8] {'ctx'}, dimensions={0}, use_global_device_ids=true | all-gather | bytes 4608 | tf_op jit(solution)/shard_map/all_gather | solution.py:75
  109.9 8.6 %all_gather.76 = bf16[72,576]{0,1:T(8,128)(2,1)S(1)} all-gather(bf16[72,144]{0,1:T(8,128)(2,1)S(1)} %copy.126), channel_id=1, replica_groups=mesh['dp'=4,'ctx'=8] {'dp'}, dimensions={1}, use_global_device_ids=true | all-gather | bytes 103680 | tf_op jit(solution)/shard_map/all_gather | solution.py:51
  118.6 7.6 %all_gather.74 = bf16[72,576]{0,1:T(8,128)(2,1)S(1)} all-gather(bf16[72,144]{0,1:T(8,128)(2,1)S(1)} %copy.122), channel_id=1, replica_groups=mesh['dp'=4,'ctx'=8] {'dp'}, dimensions={1}, use_global_device_ids=true | all-gather | bytes 103680 | tf_op jit(solution)/shard_map/all_gather | solution.py:48
  126.4 18.2 %all_gather.75 = bf16[576,576]{1,0:T(8,128)(2,1)S(1)} all-gather(bf16[72,576]{1,0:T(8,128)(2,1)S(1)} %copy.123), channel_id=1, replica_groups=mesh['dp'=4,'ctx'=8] {'ctx'}, dimensions={0}, use_global_device_ids=true | all-gather | bytes 746496 | tf_op jit(solution)/shard_map/all_gather | solution.py:57
  146.1 18.0 %all_gather.77 = bf16[576,576]{1,0:T(8,128)(2,1)} all-gather(bf16[72,576]{1,0:T(8,128)(2,1)S(1)} %copy.127), channel_id=1, replica_groups=mesh['dp'=4,'ctx'=8] {'ctx'}, dimensions={0}, use_global_device_ids=true | all-gather | bytes 746496 | tf_op jit(solution)/shard_map/all_gather | solution.py:60
  164.2 1.6 copy.181
  165.8 11.4 %while.37 = (s32[]{:T(128)}, f32[3,3,256]{2,1,0:T(4,128)S(1)}, f32[3,3,256]{2,1,0:T(4,128)S(1)}, bf16[256]{0:T(256)(128)(2,1)S(1)}, bf16[2,1024]{1,0:T(2,128)(2,...) while((s32[]{:T(128)}, f32[3,3,256]{2,1,0:T(4,128)S(1)}, ...), condition=%wide.region_4.5_spmd.clone, body=%wide.region_1.4_spmd.clone.sunk | while | flops 322187776 | bytes 22845084 | solution.py:128
  167.8 1.6 fusion.153
  169.4 2.2 select_reduce_fusion.2
  173.4 1.6 fusion.153
  175.0 2.2 select_reduce_fusion.2
  177.3 11.4 %while.38 = (s32[]{:T(128)}, f32[256,3,3,64]{0,3,2,1:T(8,128)}, bf16[2,1024,384]{1,2,0:T(8,128)(2,1)S(1)}, bf16[256]{0:T(256)(128)(2,1)S(1)}, bf16[2,1024]{1,0:T...) while((s32[]{:T(128)}, f32[256,3,3,64]{0,3,2,1:T(8,128)}, ...), condition=%wide.region_6.7_spmd.clone, body=%wide.region_5.6_spmd.clone.sunk | while | flops 615023872 | bytes 5957275 | solution.py:149
  179.1 3.4 fusion.160
  184.2 4.5 fusion.160
  189.8 1.6 multiply_reduce_fusion.2
  191.6 3.6 fusion.73
  195.2 3.5 fusion.72
  198.7 4.7 multiply_convert_fusion
  204.1 1.4 copy-done.10
  208.2 1.6 fusion.49
  211.1 33.5 %while.39 = (s32[]{:T(128)}, f32[256,3,3,64]{0,3,2,1:T(8,128)}, f32[2,1024,384]{2,1,0:T(8,128)}, bf16[2,1024,384]{1,2,0:T(8,128)(2,1)S(1)}, bf16[256]{0:T(256)(1...) while((s32[]{:T(128)}, f32[256,3,3,64]{0,3,2,1:T(8,128)}, ...), condition=%wide.region_10.11_spmd.clone, body=%wide.region_9.10_spmd.clone.sunk | while | flops 1535542528 | bytes 73576176 | solution.py:203
  213.2 1.4 fusion.172
  214.6 2.9 fusion.175
  217.5 4.0 fusion.173
  221.5 1.8 fusion.174
  223.3 1.5 fusion.176
  229.3 1.4 fusion.172
  230.7 2.9 fusion.175
  233.6 4.0 fusion.173
  237.7 2.8 fusion.174
  240.5 1.5 fusion.176
  246.1 2.6 fusion.61
  248.7 2.5 copy.131
  251.3 1.6 convert_element_type.157
  252.9 28.6 %reduce-scatter.46.cloned.1.call-done = f32[72,576]{1,0:T(8,128)} async-done(((f32[576,576]{1,0:T(8,128)}), f32[72,576]{1,0:T(8,128)}) %reduce-scatter.46.cloned.1.call-update) | async-done | bytes 165904
  281.5 1.6 convert_element_type.151
  283.2 2.5 fusion.76
  285.8 2.4 fusion.75
  288.3 2.7 fusion.77
  291.1 31.2 %reduce-scatter.28.cloned.1.call-done = f32[256,384]{0,1:T(8,128)} async-done(((f32[2048,384]{0,1:T(8,128)}), f32[256,384]{0,1:T(8,128)}) %reduce-scatter.28.cloned.1.call-update) | async-done | bytes 393232 | tf_op jit(solution)/shard_map/reduce_scatter | solution.py:307
  324.6 2.0 fusion.52
  330.5 3.2 fusion.36
  333.8 34.3 %all-reduce.12.cloned.1.call-done = (bf16[72,576]{1,0:T(8,128)(2,1)}, bf16[72,576]{1,0:T(8,128)(2,1)}) async-done(((bf16[72,576]{1,0:T(8,128)(2,1)}, bf16[72,576]{1,0:T(8,128)(2,1)}), (bf16[72,576]{1,0:T(8,128)(2,1)}, bf16[72,576]{1,0:T(8,128)(2,1)})) %all-reduce.12.cloned.1.call-update) | async-done | bytes 165904
  368.1 1.6 dynamic-slice_convert_fusion
  370.8 43.7 %reduce-scatter.36.cloned.1.call-done = f32[72,1536]{1,0:T(8,128)} async-done(((f32[576,1536]{1,0:T(8,128)}), f32[72,1536]{1,0:T(8,128)}) %reduce-scatter.36.cloned.1.call-update) | async-done | bytes 442384 | tf_op jit(solution)/shard_map/reduce_scatter | solution.py:342
  417.7 41.3 %reduce-scatter.34.cloned.1.call-done = f32[72,1536]{1,0:T(8,128)} async-done(((f32[576,1536]{1,0:T(8,128)}), f32[72,1536]{1,0:T(8,128)}) %reduce-scatter.34.cloned.1.call-update) | async-done | bytes 442384 | tf_op jit(solution)/shard_map/reduce_scatter | solution.py:341
  461.1 15.3 %all-reduce = bf16[2,576]{1,0:T(2,128)(2,1)S(1)} all-reduce(f32[2,576]{1,0:T(2,128)S(1)} %pad_maximum_fusion.5), channel_id=3, replica_groups=mesh['dp'=4,'ctx'=8] {'ctx'}, use_global_device_ids=true, to_apply=%region_15.16.clone | all-reduce | flops 1152 | bytes 6912
  476.6 31.2 %reduce-scatter.38.cloned.1.call-done = f32[192,576]{1,0:T(8,128)} async-done(((f32[1536,576]{1,0:T(8,128)}), f32[192,576]{1,0:T(8,128)}) %reduce-scatter.38.cloned.1.call-update) | async-done | bytes 442384 | tf_op jit(solution)/shard_map/reduce_scatter | solution.py:343
  510.7 28.6 %reduce-scatter.30.cloned.1.call-done = f32[72,192]{1,0:T(8,128)} async-done(((f32[576,192]{1,0:T(8,128)}), f32[72,192]{1,0:T(8,128)}) %reduce-scatter.30.cloned.1.call-update) | async-done | bytes 55312 | tf_op jit(solution)/shard_map/reduce_scatter | solution.py:338
  540.2 30.7 %reduce-scatter.32.cloned.1.call-done = f32[72,192]{1,0:T(8,128)} async-done(((f32[576,192]{1,0:T(8,128)}), f32[72,192]{1,0:T(8,128)}) %reduce-scatter.32.cloned.1.call-update) | async-done | bytes 55312 | tf_op jit(solution)/shard_map/reduce_scatter | solution.py:339
  571.8 17.5 %all-reduce.8 = (bf16[2,288]{1,0:T(2,128)(2,1)S(1)}, bf16[72,192]{1,0:T(8,128)(2,1)S(1)}, bf16[72,192]{1,0:T(8,128)(2,1)S(1)}) all-reduce(bf16[2,288]{1,0:T(2,128)(2,1)S(1)} %convert_element_type.149, bf16[72,192]{1,0:T(8,128)(2,1)S(1)} %convert_element_type.153, ...), channel_id=4, replica_groups=mesh['dp'=4,'ctx'=8] {'dp'}, use_global_device_ids=true, to_apply=%region_16.17.clone | all-reduce | flops 28224 | bytes 112896
  591.4 5.0 reduce-scatter.42.cloned.1.call-done
  598.1 25.7 %reduce-scatter.40.cloned.1.call-done = bf16[384,72]{1,0:T(8,128)(2,1)} async-done(((bf16[1536,72]{1,0:T(8,128)(2,1)}), bf16[384,72]{1,0:T(8,128)(2,1)}) %reduce-scatter.40.cloned.1.call-update) | async-done | bytes 55312
  625.5 25.4 %reduce-scatter.44.cloned.1.call-done = bf16[144,192]{1,0:T(8,128)(2,1)} async-done(((bf16[576,192]{1,0:T(8,128)(2,1)}), bf16[144,192]{1,0:T(8,128)(2,1)}) %reduce-scatter.44.cloned.1.call-update) | async-done | bytes 55312
  (267 shorter events, 52.2 us)
Async XLA Ops:
  7.2 65.4 %copy-start.36 = (bf16[72,384]{1,0:T(8,128)(2,1)S(1)}, bf16[72,384]{1,0:T(8,128)(2,1)}, u32[]{:S(2)}) copy-start(bf16[72,384]{1,0:T(8,128)(2,1)} %param.27) | copy-start | bytes 165892
  7.2 74.4 %copy-start.37 = (bf16[72,384]{1,0:T(8,128)(2,1)S(1)}, bf16[72,384]{1,0:T(8,128)(2,1)}, u32[]{:S(2)}) copy-start(bf16[72,384]{1,0:T(8,128)(2,1)} %param.26) | copy-start | bytes 165892
  7.2 84.3 %copy-start.35 = (bf16[192,144]{0,1:T(8,128)(2,1)S(1)}, bf16[192,144]{0,1:T(8,128)(2,1)}, u32[]{:S(2)}) copy-start(bf16[192,144]{0,1:T(8,128)(2,1)} %param.28) | copy-start | bytes 165892
  7.2 157.0 %all-gather.7.cloned.1.call-start = ((), (), s32[]{:S(2)}) async-start(), calls=%async_computation.11 | async-start | bytes 1769472 | tf_op jit(solution)/shard_map/all_gather | solution.py:74
  9.0 91.6 %copy-start.44 = (s32[256]{0:T(256)S(1)}, s32[256]{0:T(256)}, u32[]{:S(2)}) copy-start(s32[256]{0:T(256)} %param.19) | copy-start | bytes 3076
  9.0 100.6 %copy-start.41 = (bf16[72,144]{1,0:T(8,128)(2,1)S(1)}, bf16[72,144]{1,0:T(8,128)(2,1)}, u32[]{:S(2)}) copy-start(bf16[72,144]{1,0:T(8,128)(2,1)} %param.22) | copy-start | bytes 62212
  9.0 135.5 %copy-start.38 = (f32[256]{0:T(256)}, f32[256]{0:T(256)S(1)}, u32[]{:S(2)}) copy-start(f32[256]{0:T(256)S(1)} %add_rsqrt_fusion.1) | copy-start | bytes 3076
  22.6 87.2 %copy-start.42 = (bf16[72,144]{1,0:T(8,128)(2,1)S(1)}, bf16[72,144]{1,0:T(8,128)(2,1)}, u32[]{:S(2)}) copy-start(bf16[72,144]{1,0:T(8,128)(2,1)} %param.25) | copy-start | bytes 62212
  22.7 121.8 %copy-start.32 = (f32[576]{0:T(1024)}, f32[576]{0:T(1024)S(1)}, u32[]{:S(2)}) copy-start(f32[576]{0:T(1024)S(1)} %get-tuple-element.566) | copy-start | bytes 6916
  53.7 14.3 %copy-start.23 = (bf16[576,192]{1,0:T(8,128)(2,1)}, bf16[576,192]{1,0:T(8,128)(2,1)S(1)}, u32[]{:S(2)}) copy-start(bf16[576,192]{1,0:T(8,128)(2,1)S(1)} %all_gather.71) | copy-start | bytes 663556
  68.0 1.5 copy-start.25
  69.4 76.0 %copy-start.2 = (bf16[256,576]{0,1:T(8,128)(2,1)S(1)}, bf16[256,576]{0,1:T(8,128)(2,1)}, u32[]{:S(2)}) copy-start(bf16[256,576]{0,1:T(8,128)(2,1)} %param.18) | copy-start | bytes 884740
  71.7 74.3 %copy-start.29 = (f32[256,32]{0,1:T(8,128)}, f32[256,32]{0,1:T(8,128)S(1)}, u32[]{:S(2)}) copy-start(f32[256,32]{0,1:T(8,128)S(1)} %get-tuple-element.651) | copy-start | bytes 98308
  72.5 119.1 %all-gather.11.cloned.1.call-start = ((), (), s32[]{:S(2)}) async-start(), calls=%async_computation.13 | async-start | bytes 1990656 | tf_op jit(solution)/shard_map/all_gather | solution.py:62
  81.5 113.7 %all-gather.9.cloned.1.call-start = ((), (), s32[]{:S(2)}) async-start(), calls=%async_computation.12 | async-start | bytes 1990656 | tf_op jit(solution)/shard_map/all_gather | solution.py:61
  91.5 107.2 %all-gather.13.cloned.1.call-start = ((), (), s32[]{:S(2)}) async-start(), calls=%async_computation.14 | async-start | bytes 2211840 | tf_op jit(solution)/shard_map/all_gather | solution.py:63
  100.5 150.7 %reduce-scatter.48.cloned.1.call-start = ((), (), s32[]{:S(2)}) async-start(), calls=%async_computation.25 | async-start | bytes 1658880
  191.4 15.5 %copy-start.4 = (f32[256,576]{0,1:T(8,128)}, f32[256,576]{0,1:T(8,128)S(1)}, u32[]{:S(2)}) copy-start(f32[256,576]{0,1:T(8,128)S(1)} %get-tuple-element.653) | copy-start | bytes 1769476
  191.5 7.2 %copy-start.8 = (bf16[256,576]{0,1:T(8,128)(2,1)}, bf16[256,576]{0,1:T(8,128)(2,1)S(1)}, u32[]{:S(2)}) copy-start(bf16[256,576]{0,1:T(8,128)(2,1)S(1)} %multiply_convert_fusion.3) | copy-start | bytes 884740
  191.5 7.2 %copy-start.21 = (bf16[256,576]{0,1:T(8,128)(2,1)S(1)}, bf16[256,576]{0,1:T(8,128)(2,1)}, u32[]{:S(2)}) copy-start(bf16[256,576]{0,1:T(8,128)(2,1)} %param.29) | copy-start | bytes 884740
  198.7 4.7 copy-start.11
  203.5 3.4 copy-start.16
  203.5 3.4 copy-start.19
  203.5 2.0 copy-start.10
  205.5 1.6 copy-start.12
  207.1 1.1 copy-start.6
  211.0 70.5 %reduce-scatter.46.cloned.1.call-start = ((), (), s32[]{:S(2)}) async-start(), calls=%async_computation.24 | async-start | bytes 1658880
  211.1 34.8 %copy-start.30 = (f32[256,32]{0,1:T(8,128)S(1)}, f32[256,32]{0,1:T(8,128)}, u32[]{:S(2)}) copy-start(f32[256,32]{0,1:T(8,128)} %copy-done.29) | copy-start | bytes 98308
  211.1 34.8 %copy-start.31 = (f32[256,32]{0,1:T(8,128)S(1)}, f32[256,32]{0,1:T(8,128)}, u32[]{:S(2)}) copy-start(f32[256,32]{0,1:T(8,128)} %get-tuple-element.649) | copy-start | bytes 98308
  211.3 3.3 copy-start
  225.5 2.0 copy-start.1
  227.5 3.3 copy-start
  242.7 2.0 copy-start.1
  244.7 4.0 copy-start.18
  248.6 73.7 %reduce-scatter.28.cloned.1.call-start = ((), (), s32[]{:S(2)}) async-start(), calls=%async_computation.15 | async-start | bytes 3538944 | tf_op jit(solution)/shard_map/reduce_scatter | solution.py:307
  251.2 32.0 %copy-start.9 = (bf16[256,576]{0,1:T(8,128)(2,1)S(1)}, bf16[256,576]{0,1:T(8,128)(2,1)}, u32[]{:S(2)}) copy-start(bf16[256,576]{0,1:T(8,128)(2,1)} %copy-done.8) | copy-start | bytes 884740
  251.2 32.0 %copy-start.17 = (bf16[256,1536]{1,0:T(8,128)(2,1)S(1)}, bf16[256,1536]{1,0:T(8,128)(2,1)}, u32[]{:S(2)}) copy-start(bf16[256,1536]{1,0:T(8,128)(2,1)} %copy-done.16) | copy-start | bytes 2359300
  251.2 116.9 %all-reduce.12.cloned.1.call-start = ((), (), s32[]{:S(2)}) async-start(), calls=%async_computation.26 | async-start | bytes 368640
  283.1 2.7 copy-start.20
  283.1 131.3 %reduce-scatter.36.cloned.1.call-start = ((), (), s32[]{:S(2)}) async-start(), calls=%async_computation.19 | async-start | bytes 3981312 | tf_op jit(solution)/shard_map/reduce_scatter | solution.py:342
  285.7 2.6 copy-start.15
  285.8 2.6 copy-start.22
  285.8 173.2 %reduce-scatter.34.cloned.1.call-start = ((), (), s32[]{:S(2)}) async-start(), calls=%async_computation.18 | async-start | bytes 3981312 | tf_op jit(solution)/shard_map/reduce_scatter | solution.py:341
  288.3 219.5 %reduce-scatter.38.cloned.1.call-start = ((), (), s32[]{:S(2)}) async-start(), calls=%async_computation.20 | async-start | bytes 4423680 | tf_op jit(solution)/shard_map/reduce_scatter | solution.py:343
  291.0 32.4 %copy-start.3 = (bf16[256,576]{0,1:T(8,128)(2,1)S(1)}, bf16[256,576]{0,1:T(8,128)(2,1)}, u32[]{:S(2)}) copy-start(bf16[256,576]{0,1:T(8,128)(2,1)} %param.18) | copy-start | bytes 884740
  291.0 32.4 %copy-start.33 = (f32[576]{0:T(1024)S(1)}, f32[576]{0:T(1024)}, u32[]{:S(2)}) copy-start(f32[576]{0:T(1024)} %copy-done.32) | copy-start | bytes 6916
  291.0 32.4 %copy-start.39 = (f32[256]{0:T(256)S(1)}, f32[256]{0:T(256)}, u32[]{:S(2)}) copy-start(f32[256]{0:T(256)} %copy-done.38) | copy-start | bytes 3076
  291.0 35.7 %copy-start.46 = (u32[32]{0:T(128)S(1)}, u32[32]{0:T(128)}, u32[]{:S(2)}) copy-start(u32[32]{0:T(128)} %constant.84) | copy-start | bytes 388
  291.0 38.2 %copy-start.45 = (u32[32]{0:T(128)S(1)}, u32[32]{0:T(128)}, u32[]{:S(2)}) copy-start(u32[32]{0:T(128)} %constant.80) | copy-start | bytes 388
  291.0 39.5 %copy-start.43 = (f32[576]{0:T(1024)S(1)}, f32[576]{0:T(1024)}, u32[]{:S(2)}) copy-start(f32[576]{0:T(1024)} %get-tuple-element.561) | copy-start | bytes 6916
  291.0 39.5 %copy-start.5 = (f32[256,576]{0,1:T(8,128)S(1)}, f32[256,576]{0,1:T(8,128)}, u32[]{:S(2)}) copy-start(f32[256,576]{0,1:T(8,128)} %copy-done.4) | copy-start | bytes 1769476
  291.1 248.2 %reduce-scatter.30.cloned.1.call-start = ((), (), s32[]{:S(2)}) async-start(), calls=%async_computation.16 | async-start | bytes 663552 | tf_op jit(solution)/shard_map/reduce_scatter | solution.py:338
  323.4 7.1 %copy-start.28 = (bf16[256,3,64]{0,2,1:T(8,128)(2,1)}, bf16[256,3,64]{0,2,1:T(8,128)(2,1)S(1)}, u32[]{:S(2)}) copy-start(bf16[256,3,64]{0,2,1:T(8,128)(2,1)S(1)} %pad_maximum_fusion.4) | copy-start | bytes 294916
  324.5 45.2 %copy-start.26 = (bf16[576,192]{1,0:T(8,128)(2,1)S(1)}, bf16[576,192]{1,0:T(8,128)(2,1)}, u32[]{:S(2)}) copy-start(bf16[576,192]{1,0:T(8,128)(2,1)} %copy-done.25) | copy-start | bytes 663556
  324.5 246.4 %reduce-scatter.32.cloned.1.call-start = ((), (), s32[]{:S(2)}) async-start(), calls=%async_computation.17 | async-start | bytes 663552 | tf_op jit(solution)/shard_map/reduce_scatter | solution.py:339
  326.7 269.8 %reduce-scatter.42.cloned.1.call-start = ((), (), s32[]{:S(2)}) async-start(), calls=%async_computation.22 | async-start | bytes 491520
  330.5 86.3 %copy-start.14 = (bf16[576,576]{1,0:T(8,128)(2,1)S(1)}, bf16[576,576]{1,0:T(8,128)(2,1)}, u32[]{:S(2)}) copy-start(bf16[576,576]{1,0:T(8,128)(2,1)} %copy-done.13) | copy-start | bytes 1990660
  333.8 83.5 %copy-start.24 = (bf16[576,192]{1,0:T(8,128)(2,1)S(1)}, bf16[576,192]{1,0:T(8,128)(2,1)}, u32[]{:S(2)}) copy-start(bf16[576,192]{1,0:T(8,128)(2,1)} %copy-done.23) | copy-start | bytes 663556
  333.8 83.5 %copy-start.27 = (f32[256,384]{0,1:T(8,128)S(1)}, f32[256,384]{0,1:T(8,128)}, u32[]{:S(2)}) copy-start(f32[256,384]{0,1:T(8,128)} %reduce-scatter.28.cloned.1.call-done) | copy-start | bytes 1179652
  333.8 83.5 %copy-start.34 = (f32[576]{0:T(1024)S(1)}, f32[576]{0:T(1024)}, u32[]{:S(2)}) copy-start(f32[576]{0:T(1024)} %copy-done.32) | copy-start | bytes 6916
  333.8 83.5 %copy-start.40 = (f32[256]{0:T(256)S(1)}, f32[256]{0:T(256)}, u32[]{:S(2)}) copy-start(f32[256]{0:T(256)} %copy-done.38) | copy-start | bytes 3076
  416.5 207.3 %reduce-scatter.40.cloned.1.call-start = ((), (), s32[]{:S(2)}) async-start(), calls=%async_computation.21 | async-start | bytes 491520
  417.3 92.5 %copy-start.7 = (f32[256,576]{0,1:T(8,128)S(1)}, f32[256,576]{0,1:T(8,128)}, u32[]{:S(2)}) copy-start(f32[256,576]{0,1:T(8,128)} %copy-done.6) | copy-start | bytes 1769476
  461.0 189.9 %reduce-scatter.44.cloned.1.call-start = ((), (), s32[]{:S(2)}) async-start(), calls=%async_computation.23 | async-start | bytes 368640
  (1 other events, 0.9 us)
Sparse Core Ops, SparseCore 0:
  72.6 24.4 all-gather.6
  98.8 25.5 all-gather.10
  126.0 29.8 all-gather.8
  157.9 28.2 all-gather.12
  211.2 32.8 reduce-scatter.47
  248.8 32.7 reduce-scatter.45
  283.8 38.4 reduce-scatter.27
  326.5 41.5 all-reduce.11
  370.5 43.8 reduce-scatter.35
  416.6 42.2 reduce-scatter.33
  461.4 46.2 reduce-scatter.37
  510.0 29.2 reduce-scatter.29
  541.7 29.2 reduce-scatter.31
  573.8 22.6 reduce-scatter.41
  599.3 24.4 reduce-scatter.39
  626.7 24.1 reduce-scatter.43
where the time goes:
time: 661 us; the launch traced here: 659 us
  waiting for transfers between devices  326 us (49%)
  blocking collectives  180 us (27%)
  matrix products  75.3 us (11%)
  other arithmetic  32 us (5%)
  local copies, waits for them, and re-layouts  26.9 us (4%)
  between operations  17.4 us (3%)
    unnamed x22, waiting for transfers between devices  119 us
    reduce_scatter x1, waiting for transfers between devices, body(): lax.psum_scatter(up_weight_grad, 'ctx', scatter_dimension=0, tiled=True)  43.7 us
    reduce_scatter x1, waiting for transfers between devices, body(): lax.psum_scatter(gate_weight_grad, 'ctx', scatter_dimension=0, tiled=True)  41.3 us
    unnamed x2, blocking collectives  32.8 us
    reduce_scatter x1, waiting for transfers between devices, body(): lax.psum_scatter(key_value_part, 'ctx', scatter_dimension=0, tiled=True)  31.2 us
    reduce_scatter x1, waiting for transfers between devices, body(): lax.psum_scatter(down_weight_grad, 'ctx', scatter_dimension=0, tiled=True)  31.2 us
    reduce_scatter x1, waiting for transfers between devices, body(): lax.psum_scatter(value_weight_grad, 'ctx', scatter_dimension=0, tiled=True)  30.7 us
    reduce_scatter x1, waiting for transfers between devices, body(): lax.psum_scatter(key_weight_grad, 'ctx', scatter_dimension=0, tiled=True)  28.6 us
  transfers between devices with their start and end apart: 16, of which 11 were waited for; matrix products, arithmetic and copies ran while one was open for 17% of the time, Pallas kernels for 0%

commit v1 on v0

--- a/solution.py
+++ b/solution.py
@@ -384,7 +384,287 @@
     )
 
 
+def z_permute(block, shift, wrap):
+    size = lax.axis_size("ctx")
+    pairs = [
+        (c, (c + 2 * shift) % size)
+        for c in range(size)
+        if wrap or 0 <= c + 2 * shift < size
+    ]
+    return lax.ppermute(block, "ctx", pairs)
+
+
+def core_permute(block):
+    return lax.ppermute(block, "ctx", [(c, c ^ 1) for c in range(lax.axis_size("ctx"))])
+
+
+def dp_permute(block, offset):
+    size = lax.axis_size("dp")
+    return lax.ppermute(block, "dp", [(d, d ^ offset) for d in range(size)])
+
+
+def place(pieces, indices):
+    stacked = jnp.zeros((len(pieces),) + pieces[0].shape, pieces[0].dtype)
+    for piece, index in zip(pieces, indices):
+        stacked = lax.dynamic_update_index_in_dim(stacked, piece, index, 0)
+    return stacked
+
+
+def core_pair(mine, other):
+    first = lax.axis_index("ctx") % 2 == 0
+    return (jnp.where(first, mine, other), jnp.where(first, other, mine))
+
+
+def spread_gather(block):
+    depth = lax.axis_size("ctx") // 2
+    level = lax.axis_index("ctx") // 2
+    column = lax.axis_index("dp")
+    along = place(
+        [block] + [z_permute(block, s, True) for s in range(1, depth)],
+        [(level - s) % depth for s in range(depth)],
+    )
+    across = place(
+        [along] + [dp_permute(along, s) for s in range(1, lax.axis_size("dp"))],
+        [column ^ s for s in range(lax.axis_size("dp"))],
+    )
+    even, odd = core_pair(across, core_permute(across))
+    return jnp.stack([even, odd], axis=2)
+
+
+def spread_sum(blocks):
+    depth = lax.axis_size("ctx") // 2
+    level = lax.axis_index("ctx") // 2
+    core = lax.axis_index("ctx") % 2
+    column = lax.axis_index("dp")
+    kept = lax.dynamic_index_in_dim(blocks, core, 2, keepdims=False)
+    sent = lax.dynamic_index_in_dim(blocks, 1 - core, 2, keepdims=False)
+    half = (kept.astype(jnp.float32) + core_permute(sent).astype(jnp.float32)).astype(jnp.bfloat16)
+    total = lax.dynamic_index_in_dim(half, column, 0, keepdims=False).astype(jnp.float32)
+    for s in range(1, lax.axis_size("dp")):
+        part = lax.dynamic_index_in_dim(half, column ^ s, 0, keepdims=False)
+        total = total + dp_permute(part, s).astype(jnp.float32)
+    quarter = total.astype(jnp.bfloat16)
+    result = lax.dynamic_index_in_dim(quarter, level, 0, keepdims=False).astype(jnp.float32)
+    for s in range(1, depth):
+        part = lax.dynamic_index_in_dim(quarter, (level + s) % depth, 0, keepdims=False)
+        result = result + z_permute(part, s, True).astype(jnp.float32)
+    return result
+
+
+def assemble(gathered, begin, width):
+    dp, depth, cores, rows = gathered.shape[:4]
+    part = gathered[..., begin : begin + width].reshape(dp, depth * cores * rows, width)
+    return jnp.transpose(part, (1, 0, 2)).reshape(depth * cores * rows, dp * width)
+
+
+def cut(matrix):
+    dp, ctx = lax.axis_size("dp"), lax.axis_size("ctx")
+    rows, width = matrix.shape[0] // ctx, matrix.shape[1] // dp
+    blocks = matrix.astype(jnp.bfloat16).reshape(ctx // 2, 2, rows, dp, width)
+    return jnp.transpose(blocks, (3, 0, 1, 2, 4))
+
+
+def chain_gather(block):
+    depth = lax.axis_size("ctx") // 2
+    level = lax.axis_index("ctx") // 2
+    along = place(
+        [block] + [z_permute(block, s, False) for s in range(1, depth)],
+        [(level - s) % depth for s in range(depth)],
+    )
+    even, odd = core_pair(along, core_permute(along))
+    return jnp.stack([even, odd], axis=1)
+
+
+def chain_sum(blocks):
+    depth = lax.axis_size("ctx") // 2
+    level = lax.axis_index("ctx") // 2
+    core = lax.axis_index("ctx") % 2
+    kept = lax.dynamic_index_in_dim(blocks, core, 1, keepdims=False)
+    sent = lax.dynamic_index_in_dim(blocks, 1 - core, 1, keepdims=False).astype(jnp.bfloat16)
+    half = kept + core_permute(sent).astype(jnp.float32)
+    result = lax.dynamic_index_in_dim(half, level, 0, keepdims=False)
+    for s in range(1, depth):
+        part = lax.dynamic_index_in_dim(half, (level - s) % depth, 0, keepdims=False)
+        result = result + z_permute(part.astype(jnp.bfloat16), -s, False).astype(jnp.float32)
+    return result
+
+
+def staged_body(
+    tokens,
+    segment_ids,
+    positions,
+    norm_gains,
+    w_query,
+    w_key,
+    w_value,
+    w_out,
+    w_gate,
+    w_up,
+    w_down,
+    cotangent,
+):
+    first = spread_gather(jnp.concatenate([w_query, w_key, w_value, norm_gains.T], axis=1))
+    second = spread_gather(jnp.concatenate([w_out, w_gate, w_up], axis=1))
+    third = spread_gather(w_down)
+    nq, nk, ng = w_query.shape[1], w_key.shape[1], w_gate.shape[1]
+    weights = (
+        assemble(first, 0, nq),
+        assemble(first, nq, nk),
+        assemble(first, nq + nk, nk),
+        assemble(second, 0, nq),
+        assemble(second, nq, ng),
+        assemble(second, nq + ng, ng),
+        assemble(third, 0, nq),
+    )
+    gain_rows = first[0, ..., nq + 2 * nk :].reshape(-1, 2).T
+    repeat = HEADS // KV_HEADS
+    key_width = KV_HEADS * HEAD
+    logit_scale = HEAD ** (-0.5)
+    rows_here = tokens.shape[0]
+    query_index = lax.axis_index("ctx") * rows_here + jnp.arange(rows_here, dtype=jnp.int32)
+    cosine_table, sine_table = tables(positions)
+    hidden = tokens.astype(jnp.float32)
+    gain_one = gain_rows[0].astype(jnp.float32)
+    gain_two = gain_rows[1].astype(jnp.float32)
+    inverse_one = lax.rsqrt(jnp.mean(hidden * hidden, axis=1, keepdims=True) + EPSILON)
+    normed_one = (hidden * inverse_one * gain_one).astype(jnp.bfloat16)
+    queries = rotate(
+        jnp.dot(normed_one, weights[0], preferred_element_type=jnp.float32),
+        cosine_table,
+        sine_table,
+    ).astype(jnp.bfloat16)
+    key_proj = rotate(
+        jnp.dot(normed_one, weights[1], preferred_element_type=jnp.float32),
+        cosine_table,
+        sine_table,
+    ).astype(jnp.bfloat16)
+    value_proj = jnp.dot(normed_one, weights[2], preferred_element_type=jnp.float32).astype(
+        jnp.bfloat16
+    )
+    key_values = jnp.concatenate([key_proj, value_proj], axis=1)
+    segments_low = segment_ids.astype(jnp.bfloat16)
+    spare = jnp.zeros((16, 2 * key_width), jnp.bfloat16)
+    spare = spare.at[0, :rows_here].set(segments_low)
+    parts = chain_gather(jnp.concatenate([key_values, spare], axis=0))
+    gathered = (
+        parts[:, :, :rows_here].reshape(-1, 2 * key_width),
+        parts[:, :, rows_here, :rows_here].reshape(-1),
+    )
+    query_head_rows = queries.reshape(rows_here, KV_HEADS, repeat, HEAD)
+    log_total, attention_output = attend_forward(
+        query_head_rows, gathered, segments_low, query_index, logit_scale
+    )
+    attended_low = attention_output.reshape(rows_here, HEADS * HEAD).astype(jnp.bfloat16)
+    middle = hidden + jnp.dot(attended_low, weights[3], preferred_element_type=jnp.float32)
+    inverse_two = lax.rsqrt(jnp.mean(middle * middle, axis=1, keepdims=True) + EPSILON)
+    normed_two = (middle * inverse_two * gain_two).astype(jnp.bfloat16)
+    gate_out = jnp.dot(normed_two, weights[4], preferred_element_type=jnp.float32)
+    up_out = jnp.dot(normed_two, weights[5], preferred_element_type=jnp.float32)
+    inner_act = (jax.nn.silu(gate_out) * up_out).astype(jnp.bfloat16)
+    mixed_out = (
+        middle + jnp.dot(inner_act, weights[6], preferred_element_type=jnp.float32)
+    ).astype(jnp.bfloat16)
+    down_weight_grad = jnp.einsum(
+        "tf,td->fd", inner_act, cotangent, preferred_element_type=jnp.float32
+    )
+    inner_grad = jnp.einsum("td,fd->tf", cotangent, weights[6], preferred_element_type=jnp.float32)
+    sigmoid_gate = jax.nn.sigmoid(gate_out)
+    silu_gate = gate_out * sigmoid_gate
+    gate_grad_low = (
+        inner_grad * up_out * sigmoid_gate * (1.0 + gate_out * (1.0 - sigmoid_gate))
+    ).astype(jnp.bfloat16)
+    up_grad_low = (inner_grad * silu_gate).astype(jnp.bfloat16)
+    gate_weight_grad = jnp.einsum(
+        "td,tf->df", normed_two, gate_grad_low, preferred_element_type=jnp.float32
+    )
+    up_weight_grad = jnp.einsum(
+        "td,tf->df", normed_two, up_grad_low, preferred_element_type=jnp.float32
+    )
+    normed_two_grad = jnp.einsum(
+        "tf,df->td", gate_grad_low, weights[4], preferred_element_type=jnp.float32
+    )
+    normed_two_grad = normed_two_grad + jnp.einsum(
+        "tf,df->td", up_grad_low, weights[5], preferred_element_type=jnp.float32
+    )
+    middle_grad, gain_two_grad = norm_back(middle, inverse_two, gain_two, normed_two_grad)
+    middle_grad = middle_grad + cotangent.astype(jnp.float32)
+    branch_low = middle_grad.astype(jnp.bfloat16)
+    out_weight_grad = jnp.einsum(
+        "tc,td->cd", attended_low, branch_low, preferred_element_type=jnp.float32
+    )
+    attention_output_grad = jnp.einsum(
+        "td,cd->tc", branch_low, weights[3], preferred_element_type=jnp.float32
+    ).astype(jnp.bfloat16)
+    query_part, key_value_part = attend_backward(
+        query_head_rows,
+        gathered,
+        segments_low,
+        query_index,
+        logit_scale,
+        log_total,
+        attention_output,
+        attention_output_grad.reshape(rows_here, KV_HEADS, repeat, HEAD),
+    )
+    own_grads = chain_sum(
+        key_value_part.reshape(lax.axis_size("ctx") // 2, 2, rows_here, 2 * key_width)
+    )
+    query_low = rotate(
+        query_part.reshape(rows_here, HEADS * HEAD) * logit_scale, cosine_table, -sine_table
+    ).astype(jnp.bfloat16)
+    key_low = rotate(own_grads[:, :key_width] * logit_scale, cosine_table, -sine_table).astype(
+        jnp.bfloat16
+    )
+    value_low = own_grads[:, key_width:].astype(jnp.bfloat16)
+    query_weight_grad = jnp.einsum(
+        "td,tc->dc", normed_one, query_low, preferred_element_type=jnp.float32
+    )
+    key_weight_grad = jnp.einsum(
+        "td,tc->dc", normed_one, key_low, preferred_element_type=jnp.float32
+    )
+    value_weight_grad = jnp.einsum(
+        "td,tc->dc", normed_one, value_low, preferred_element_type=jnp.float32
+    )
+    normed_one_grad = jnp.einsum(
+        "tc,dc->td", query_low, weights[0], preferred_element_type=jnp.float32
+    )
+    normed_one_grad = normed_one_grad + jnp.einsum(
+        "tc,dc->td", key_low, weights[1], preferred_element_type=jnp.float32
+    )
+    normed_one_grad = normed_one_grad + jnp.einsum(
+        "tc,dc->td", value_low, weights[2], preferred_element_type=jnp.float32
+    )
+    hidden_grad, gain_one_grad = norm_back(hidden, inverse_one, gain_one, normed_one_grad)
+    token_grad = middle_grad + hidden_grad
+    gain_terms = jnp.stack([gain_one_grad, gain_two_grad])
+    down_grad = spread_sum(cut(down_weight_grad))
+    second_grad = spread_sum(
+        jnp.concatenate(
+            [cut(out_weight_grad), cut(gate_weight_grad), cut(up_weight_grad)], axis=-1
+        )
+    )
+    gain_blocks = jnp.tile(gain_terms.T, (1, lax.axis_size("dp")))
+    first_grad = spread_sum(
+        jnp.concatenate(
+            [cut(query_weight_grad), cut(key_weight_grad), cut(value_weight_grad), cut(gain_blocks)],
+            axis=-1,
+        )
+    )
+    return (
+        mixed_out,
+        token_grad,
+        first_grad[:, nq + 2 * nk :].T,
+        first_grad[:, :nq],
+        first_grad[:, nq : nq + nk],
+        first_grad[:, nq + nk : nq + 2 * nk],
+        second_grad[:, :nq],
+        second_grad[:, nq : nq + ng],
+        second_grad[:, nq + ng :],
+        down_grad,
+    )
+
+
 def solution(mesh):
+    dp, ctx = mesh.shape["dp"], mesh.shape["ctx"]
     placed = (
         P(("dp", "ctx"), None),
         P(("dp", "ctx")),
@@ -400,7 +680,7 @@
         P(("dp", "ctx"), None),
     )
     return jax.shard_map(
-        body,
+        staged_body if dp == 4 and ctx == 8 else body,
         mesh=mesh,
         in_specs=placed,
         out_specs=(

time: 661 us -> 382 us (0.58)
  waiting for transfers between devices: 326 us -> 96.4 us
  blocking collectives: 180 us -> 0 us
  local copies, waits for them, and re-layouts: 26.9 us -> 108 us
  starting transfers between devices: 0.93 us -> 70 us
  matrix products: 75.3 us -> 51.9 us
  between operations: 17.4 us -> 2.24 us
  other arithmetic: 32 us -> 45.9 us
    reduce_scatter x6 -> x0, waiting for transfers between devices: 207 us -> none  [the longest x1 43.7 us: body(): lax.psum_scatter(up_weight_grad, 'ctx', scatter_dimension=0, tiled=True)]
    all_gather x13 -> x0, blocking collectives: 147 us -> none  [the longest x1 18.2 us: gather_weights(): lax.all_gather(widened[0], 'ctx', axis=0, tiled=True)]
    unnamed x22 -> x0, waiting for transfers between devices: 119 us -> none
    ppermute x0 -> x50, waiting for transfers between devices: none -> 96.4 us  [the longest x18 62.6 us: dp_permute(): return lax.ppermute(block, 'dp', [(d, d ^ offset) for d in range(size)])]
    ppermute x0 -> x50, starting transfers between devices: none -> 70 us  [the longest x24 43.4 us: z_permute(): return lax.ppermute(block, 'ctx', pairs)]
    reshape x3 -> x18, local copies, waits for them, and re-layouts: 4.06 us -> 39.6 us  [the longest x11 27.5 us: cut(): blocks = matrix.astype(jnp.bfloat16).reshape(ctx // 2, 2, rows, dp, width)]
    unnamed x2 -> x0, blocking collectives: 32.8 us -> none
    dot_general x21, matrix products: 40.1 us -> 20 us  [the longest x1 2.35 us: staged_body(): jnp.einsum('td,fd->tf', cotangent, weights[6], preferred_element_type=jnp...]
  transfers between devices with their start and end apart: 16 -> 50, of which waited for: 11 -> 24; matrix products, arithmetic and copies ran while one was open for 17% -> 36% of each run, Pallas kernels for 0% -> 0%
where the time goes in v1:
time: 382 us; the launch traced here: 376 us
  local copies, waits for them, and re-layouts  108 us (28%)
  waiting for transfers between devices  96.4 us (25%)
  starting transfers between devices  70 us (18%)
  matrix products  51.9 us (14%)
  other arithmetic  45.9 us (12%)
    ppermute x18, waiting for transfers between devices, dp_permute(): return lax.ppermute(block, 'dp', [(d, d ^ offset) for d in range(size)])  62.6 us
    ppermute x24, starting transfers between devices, z_permute(): return lax.ppermute(block, 'ctx', pairs)  43.4 us
    ppermute x24, waiting for transfers between devices, z_permute(): return lax.ppermute(block, 'ctx', pairs)  33.8 us
    reshape x11, local copies, waits for them, and re-layouts, cut(): blocks = matrix.astype(jnp.bfloat16).reshape(ctx // 2, 2, rows, dp, width)  27.5 us
    ppermute x18, starting transfers between devices, dp_permute(): return lax.ppermute(block, 'dp', [(d, d ^ offset) for d in range(size)])  24.9 us
    unnamed x103, local copies, waits for them, and re-layouts  15.4 us
    reshape x5, local copies, waits for them, and re-layouts, assemble(): gathered[..., begin:begin + width].reshape(dp, depth * cores * rows, width)  9.27 us
    dot_general x2, matrix products, out_step(): jnp.einsum('ejfy,yex->fejx', softmax_reduced, value_head_rows, preferred_...  7.88 us
  transfers between devices with their start and end apart: 50, of which 24 were waited for; matrix products, arithmetic and copies ran while one was open for 36% of the time, Pallas kernels for 0%

profile of v1, /device:TPU:0, one launch (start us, length us, event | category | flops | bytes accessed | tf_op | source)
XLA Modules:
  0.0 375.7 jit_solution(4124088519795856504)
XLA Ops:
  0.7 3.1 collective-permute-start.18
  3.8 2.1 collective-permute-start.20
  10.1 2.0 collective-permute-start.1
  17.9 3.0 collective-permute-start.2
  21.0 1.8 collective-permute-done.2
  23.5 3.8 %collective-permute-start.13 = (bf16[72,912]{1,0:T(8,128)(2,1)S(1)}, bf16[72,912]{1,0:T(8,128)(2,1)S(1)}, u32[]{:S(2)}, u32[]{:S(2)}) collective-permute-start(bf16[72,912]{1,0:T(8,128)(2,1)S(1)} %pad_maximum_fusion.9), channel_id=1, source_target_pairs={{0,6},{1,7},{2,0},{3,1},{4,2},{5,3},{6,4},{7,5},{8,14},{9,15},{10,... | collective-permute-start | bytes 393992 | tf_op jit(solution)/shard_map/ppermute | solution.py:394
  27.3 2.7 collective-permute-start.5
  32.1 2.4 collective-permute-start.23
  39.9 2.0 collective-permute-done.4
  43.0 2.1 collective-permute-start.15
  45.1 5.9 %collective-permute-done.21 = bf16[4,192,144]{1,2,0:T(8,128)(2,1)S(1)} collective-permute-done((bf16[4,192,144]{1,2,0:T(8,128)(2,1)S(1)}, bf16[4,192,144]{1,2,0:T(8,128)(2,1)S(1)}, u32[]{:S(2)}, u32[]{:S(2)}) %collective-permute-start.21) | collective-permute-done | bytes 221216 | tf_op jit(solution)/shard_map/ppermute | solution.py:403
  52.5 8.3 %collective-permute-done.22 = bf16[4,192,144]{1,2,0:T(8,128)(2,1)S(1)} collective-permute-done((bf16[4,192,144]{1,2,0:T(8,128)(2,1)S(1)}, bf16[4,192,144]{1,2,0:T(8,128)(2,1)S(1)}, u32[]{:S(2)}, u32[]{:S(2)}) %collective-permute-start.22) | collective-permute-done | bytes 221216 | tf_op jit(solution)/shard_map/ppermute | solution.py:403
  61.5 11.6 %collective-permute-done.14 = bf16[4,72,912]{2,1,0:T(8,128)(2,1)S(1)} collective-permute-done((bf16[4,72,912]{2,1,0:T(8,128)(2,1)S(1)}, bf16[4,72,912]{2,1,0:T(8,128)(2,1)S(1)}, u32[]{:S(2)}, u32[]{:S(2)}) %collective-permute-start.14) | collective-permute-done | bytes 525344 | tf_op jit(solution)/shard_map/ppermute | solution.py:403
  80.8 8.4 %collective-permute-start.8 = (bf16[272,384]{0,1:T(8,128)(2,1)}, bf16[272,384]{0,1:T(8,128)(2,1)}, u32[]{:S(2)}, u32[]{:S(2)}) collective-permute-start(bf16[272,384]{0,1:T(8,128)(2,1)} %get-tuple-element.589), channel_id=1, source_target_pairs={{0,4},{1,5},{2,6},{3,7},{8,12},{9,13},{10,14},{11,15},{16,20},{17,... | collective-permute-start | bytes 626696 | tf_op jit(solution)/shard_map/ppermute | solution.py:394
  89.2 2.0 collective-permute-start.7
  91.2 2.3 collective-permute-start.9
  93.5 3.8 %copy.181 = bf16[4,4,2,72,144]{3,2,1,4,0:T(2,128)(2,1)} copy(bf16[4,4,2,72,144]{4,3,1,0,2:T(8,128)(2,1)} %pad_maximum_fusion.4) | data formatting | bytes 1327104 | tf_op jit(solution)/shard_map/slice | solution.py:456
  97.3 4.3 %reshape.329 = bf16[4,576,144]{1,2,0:T(8,128)(2,1)S(1)} reshape(bf16[4,4,2,72,144]{3,2,1,4,0:T(2,128)(2,1)} %copy.181) | data formatting | bytes 1327104 | tf_op jit(solution)/shard_map/reshape | solution.py:456
  106.4 2.1 collective-permute-done.9
  113.7 1.8 copy.188
  115.5 2.9 reshape.337
  123.3 11.7 %while.38 = (s32[]{:T(128)}, f32[3,3,256]{2,1,0:T(4,128)S(1)}, f32[3,3,256]{2,1,0:T(4,128)S(1)}, bf16[256]{0:T(256)(128)(2,1)S(1)}, bf16[2,1024]{1,0:T(2,128)(2,...) while((s32[]{:T(128)}, f32[3,3,256]{2,1,0:T(4,128)S(1)}, ...), condition=%wide.region_4.5_spmd.clone, body=%wide.region_1.4_spmd.clone.sunk | while | flops 322187776 | bytes 22845084 | solution.py:128
  127.1 2.2 select_reduce_fusion.2
  132.7 2.2 select_reduce_fusion.2
  135.0 11.4 %while.39 = (s32[]{:T(128)}, f32[256,3,3,64]{0,3,2,1:T(8,128)}, bf16[2,1024,384]{1,2,0:T(8,128)(2,1)S(1)}, bf16[256]{0:T(256)(128)(2,1)S(1)}, bf16[2,1024]{1,0:T...) while((s32[]{:T(128)}, f32[256,3,3,64]{0,3,2,1:T(8,128)}, ...), condition=%wide.region_6.7_spmd.clone, body=%wide.region_5.6_spmd.clone.sunk | while | flops 615023872 | bytes 5957275 | solution.py:149
  136.8 3.4 fusion.184
  141.9 4.5 %fusion.184 = f32[256,3,3,64]{0,3,2,1:T(8,128)} fusion(bf16[1024,3,64,1]{0,2,3,1:T(8,128)(2,1)S(1)} %bitcast.480, f32[3,3,256]{2,1,0:T(4,128)S(1)} %get-tuple-element.864, pred[256,1024]{0,1:T(8,128)(4,1)S(1)} %compare_and_fusion.7, bf16[1024,3,64,1]{0,2,3,1:T(8,128)(2,1)S(1)} %bitcast.479, bf16[256,3,3,64]{0,3,2,1:T(8,128)(2,1)S(1)} %get-tuple-element.863, ...), kind=kOutput, calls=%fused_computation.22.clone.1 | convolution fusion | flops 613711872 | bytes 2532353 | tf_op jit(solution)/shard_map/while/body/eval_jaxpr/ejfy,yex->fejx/dot_general | solution.py:140
  148.2 2.7 select_bitcast_fusion.1
  151.0 2.3 pad_maximum_fusion.3
  162.5 2.4 multiply_convert_fusion
  171.0 1.8 convolution_convert_fusion.2
  173.0 3.9 %reshape.344 = bf16[4,2,72,4,144]{4,3,2,1,0:T(4,128)(2,1)} reshape(bf16[576,576]{1,0:T(8,128)(2,1)} %convolution_convert_fusion.3) | data formatting | bytes 1327104 | tf_op jit(solution)/shard_map/reshape | solution.py:463
  178.4 1.8 convolution_convert_fusion
  180.3 7.2 %reshape.347 = bf16[4,2,192,4,144]{2,1,0,4,3:T(2,128)(2,1)} reshape(bf16[1536,576]{0,1:T(8,128)(2,1)} %convolution_convert_fusion) | data formatting | bytes 3538944 | tf_op jit(solution)/shard_map/reshape | solution.py:463
  187.4 4.1 %reshape.346 = bf16[4,2,72,4,384]{4,3,2,1,0:T(4,128)(2,1)} reshape(bf16[576,1536]{1,0:T(8,128)(2,1)} %convolution_convert_fusion.1) | data formatting | bytes 3538944 | tf_op jit(solution)/shard_map/reshape | solution.py:463
  191.5 4.1 %reshape.345 = bf16[4,2,72,4,384]{4,3,2,1,0:T(4,128)(2,1)} reshape(bf16[576,1536]{1,0:T(8,128)(2,1)} %convolution_convert_fusion.2) | data formatting | bytes 3538944 | tf_op jit(solution)/shard_map/reshape | solution.py:463
  195.6 2.5 copy_bitcast_fusion
  198.1 3.1 pad_maximum_fusion
  204.5 6.3 %constant_dynamic-slice_fusion.1 = (bf16[4,1,192,4,144]{2,1,0,4,3:T(2,128)(2,1)}, bf16[4,1,192,4,144]{2,1,0,4,3:T(2,128)(2,1)S(1)}) fusion(bf16[4,2,192,4,144]{2,1,0,4,3:T(2,128)(2,1)S(1)} %copy-done.2, s32[]{:T(128)S(6)} %select_n.299, s32[]{:T(128)S(6)} %select_n.300), kind=kLoop, calls=%fused_computation.233 | loop fusion | bytes 3538952 | tf_op jit(solution)/shard_map/jit(dynamic_index_in_dim)/dynamic_slice | solution.py:439
  212.7 30.4 %while.40 = (s32[]{:T(128)}, f32[256,3,3,64]{0,3,2,1:T(8,128)}, f32[2,1024,384]{2,1,0:T(8,128)}, bf16[2,1024,384]{1,2,0:T(8,128)(2,1)S(1)}, bf16[256]{0:T(256)(1...) while((s32[]{:T(128)}, f32[256,3,3,64]{0,3,2,1:T(8,128)}, ...), condition=%wide.region_10.11_spmd.clone, body=%wide.region_9.10_spmd.clone.sunk | while | flops 1535542528 | bytes 74755840 | solution.py:203
  216.4 2.0 fusion.199
  218.4 3.3 fusion.197
  230.9 2.0 fusion.199
  232.8 3.2 fusion.197
  236.1 2.9 fusion.198
  250.8 2.7 constant_dynamic-slice_fusion.3
  253.5 3.2 copy.192
  265.3 6.5 %collective-permute-done.26 = bf16[256,384]{0,1:T(8,128)(2,1)S(1)} collective-permute-done((bf16[256,384]{0,1:T(8,128)(2,1)S(1)}, bf16[256,384]{0,1:T(8,128)(2,1)S(1)}, u32[]{:S(2)}, u32[]{:S(2)}) %collective-permute-start.26) | collective-permute-done | bytes 196640 | tf_op jit(solution)/shard_map/ppermute | solution.py:394
  271.8 8.3 %collective-permute-done.28 = bf16[256,384]{0,1:T(8,128)(2,1)S(1)} collective-permute-done((bf16[256,384]{0,1:T(8,128)(2,1)S(1)}, bf16[256,384]{0,1:T(8,128)(2,1)S(1)}, u32[]{:S(2)}, u32[]{:S(2)}) %collective-permute-start.28) | collective-permute-done | bytes 196640 | tf_op jit(solution)/shard_map/ppermute | solution.py:394
  280.1 6.2 %collective-permute-done.27 = bf16[256,384]{0,1:T(8,128)(2,1)S(1)} collective-permute-done((bf16[256,384]{0,1:T(8,128)(2,1)S(1)}, bf16[256,384]{0,1:T(8,128)(2,1)S(1)}, u32[]{:S(2)}, u32[]{:S(2)}) %collective-permute-start.27) | collective-permute-done | bytes 196640 | tf_op jit(solution)/shard_map/ppermute | solution.py:394
  289.1 2.2 copy.195
  294.7 2.4 pad_maximum_fusion.6
  303.4 3.8 %collective-permute-done.44 = bf16[4,192,144]{1,2,0:T(8,128)(2,1)S(1)} collective-permute-done((bf16[4,192,144]{1,2,0:T(8,128)(2,1)S(1)}, bf16[4,192,144]{1,2,0:T(8,128)(2,1)S(1)}, u32[]{:S(2)}, u32[]{:S(2)}) %collective-permute-start.44) | collective-permute-done | bytes 221216 | tf_op jit(solution)/shard_map/ppermute | solution.py:403
  307.2 2.2 collective-permute-start.32
  309.4 4.9 %collective-permute-done.46 = bf16[4,192,144]{1,2,0:T(8,128)(2,1)S(1)} collective-permute-done((bf16[4,192,144]{1,2,0:T(8,128)(2,1)S(1)}, bf16[4,192,144]{1,2,0:T(8,128)(2,1)S(1)}, u32[]{:S(2)}, u32[]{:S(2)}) %collective-permute-start.46) | collective-permute-done | bytes 221216 | tf_op jit(solution)/shard_map/ppermute | solution.py:403
  316.8 2.6 collective-permute-start.49
  320.3 2.2 collective-permute-done.31
  322.7 3.8 %collective-permute-start.35 = (bf16[72,242]{1,0:T(8,128)(2,1)S(1)}, bf16[72,242]{1,0:T(8,128)(2,1)S(1)}, u32[]{:S(2)}, u32[]{:S(2)}) collective-permute-start(bf16[72,242]{1,0:T(8,128)(2,1)S(1)} %get-tuple-element.594), channel_id=1, source_target_pairs={{0,6},{1,7},{2,0},{3,1},{4,2},{5,3},{6,4},{7,5},{8,14},{9,15},{10,... | collective-permute-start | bytes 104552 | tf_op jit(solution)/shard_map/ppermute | solution.py:394
  326.5 2.8 fusion.35
  337.9 9.0 %collective-permute-done.37 = bf16[4,72,912]{2,1,0:T(8,128)(2,1)} collective-permute-done((bf16[4,72,912]{2,1,0:T(8,128)(2,1)}, bf16[4,72,912]{2,1,0:T(8,128)(2,1)}, u32[]{:S(2)}, u32[]{:S(2)}) %collective-permute-start.37) | collective-permute-done | bytes 525344 | tf_op jit(solution)/shard_map/ppermute | solution.py:403
  347.0 10.4 %collective-permute-done.39 = bf16[4,72,912]{2,1,0:T(8,128)(2,1)} collective-permute-done((bf16[4,72,912]{2,1,0:T(8,128)(2,1)S(1)}, bf16[4,72,912]{2,1,0:T(8,128)(2,1)}, u32[]{:S(2)}, u32[]{:S(2)}) %collective-permute-start.39) | collective-permute-done | bytes 525344 | tf_op jit(solution)/shard_map/ppermute | solution.py:403
  358.6 1.8 fusion.42
  361.0 3.3 collective-permute-start.42
  369.0 5.0 %collective-permute-done.41 = bf16[72,912]{1,0:T(8,128)(2,1)S(1)} collective-permute-done((bf16[72,912]{1,0:T(8,128)(2,1)S(1)}, bf16[72,912]{1,0:T(8,128)(2,1)S(1)}, u32[]{:S(2)}, u32[]{:S(2)}) %collective-permute-start.41) | collective-permute-done | bytes 131360 | tf_op jit(solution)/shard_map/ppermute | solution.py:394
  (396 shorter events, 142.6 us)
Async XLA Ops:
  0.6 15.2 %copy-start.40 = (bf16[72,384]{1,0:T(8,128)(2,1)S(1)}, bf16[72,384]{1,0:T(8,128)(2,1)}, u32[]{:S(2)}) copy-start(bf16[72,384]{1,0:T(8,128)(2,1)} %param.29) | copy-start | bytes 165892
  0.7 15.2 %copy-start.41 = (bf16[72,384]{1,0:T(8,128)(2,1)S(1)}, bf16[72,384]{1,0:T(8,128)(2,1)}, u32[]{:S(2)}) copy-start(bf16[72,384]{1,0:T(8,128)(2,1)} %param.28) | copy-start | bytes 165892
  0.7 15.2 %copy-start.44 = (bf16[72,144]{1,0:T(8,128)(2,1)S(1)}, bf16[72,144]{1,0:T(8,128)(2,1)}, u32[]{:S(2)}) copy-start(bf16[72,144]{1,0:T(8,128)(2,1)} %param.27) | copy-start | bytes 62212
  0.7 16.2 %copy-start.47 = (s32[256]{0:T(256)S(1)}, s32[256]{0:T(256)}, u32[]{:S(2)}) copy-start(s32[256]{0:T(256)} %param.21) | copy-start | bytes 3076
  0.7 22.8 %collective-permute-start.18 = (bf16[192,144]{0,1:T(8,128)(2,1)}, bf16[192,144]{0,1:T(8,128)(2,1)S(1)}, u32[]{:S(2)}, u32[]{:S(2)}) collective-permute-start(bf16[192,144]{0,1:T(8,128)(2,1)} %param.30), channel_id=1, source_target_pairs={{0,2},{1,3},{2,4},{3,5},{4,6},{5,7},{6,0},{7,1},{8,10},{9,11},{10,... | collective-permute-start | bytes 165896 | tf_op jit(solution)/shard_map/ppermute | solution.py:394
  3.8 26.3 %collective-permute-start.20 = (bf16[192,144]{0,1:T(8,128)(2,1)}, bf16[192,144]{0,1:T(8,128)(2,1)S(1)}, u32[]{:S(2)}, u32[]{:S(2)}) collective-permute-start(bf16[192,144]{0,1:T(8,128)(2,1)} %param.30), channel_id=1, source_target_pairs={{0,6},{1,7},{2,0},{3,1},{4,2},{5,3},{6,4},{7,5},{8,14},{9,15},{10,... | collective-permute-start | bytes 165896 | tf_op jit(solution)/shard_map/ppermute | solution.py:394
  5.9 21.5 %collective-permute-start.19 = (bf16[192,144]{0,1:T(8,128)(2,1)}, bf16[192,144]{0,1:T(8,128)(2,1)S(1)}, u32[]{:S(2)}, u32[]{:S(2)}) collective-permute-start(bf16[192,144]{0,1:T(8,128)(2,1)} %param.30), channel_id=1, source_target_pairs={{0,4},{1,5},{2,6},{3,7},{4,0},{5,1},{6,2},{7,3},{8,12},{9,13},{10,... | collective-permute-start | bytes 165896 | tf_op jit(solution)/shard_map/ppermute | solution.py:394
  10.1 10.9 %collective-permute-start.1 = (bf16[72,242]{1,0:T(8,128)(2,1)S(1)}, bf16[72,242]{1,0:T(8,128)(2,1)S(1)}, u32[]{:S(2)}, u32[]{:S(2)}) collective-permute-start(bf16[72,242]{1,0:T(8,128)(2,1)S(1)} %get-tuple-element.539), channel_id=1, source_target_pairs={{0,4},{1,5},{2,6},{3,7},{4,0},{5,1},{6,2},{7,3},{8,12},{9,13},{10,... | collective-permute-start | bytes 104552 | tf_op jit(solution)/shard_map/ppermute | solution.py:394
  12.1 5.8 %collective-permute-start = (bf16[72,242]{1,0:T(8,128)(2,1)S(1)}, bf16[72,242]{1,0:T(8,128)(2,1)S(1)}, u32[]{:S(2)}, u32[]{:S(2)}) collective-permute-start(bf16[72,242]{1,0:T(8,128)(2,1)S(1)} %get-tuple-element.539), channel_id=1, source_target_pairs={{0,2},{1,3},{2,4},{3,5},{4,6},{5,7},{6,0},{7,1},{8,10},{9,11},{10,... | collective-permute-start | bytes 104552 | tf_op jit(solution)/shard_map/ppermute | solution.py:394
  13.9 87.8 %copy-start.45 = (f32[256]{0:T(256)}, f32[256]{0:T(256)S(1)}, u32[]{:S(2)}) copy-start(f32[256]{0:T(256)S(1)} %add_rsqrt_fusion.1) | copy-start | bytes 3076
  16.8 94.9 %copy-start.35 = (f32[256,32]{0,1:T(8,128)}, f32[256,32]{0,1:T(8,128)S(1)}, u32[]{:S(2)}) copy-start(f32[256,32]{0,1:T(8,128)S(1)} %get-tuple-element.600) | copy-start | bytes 98308
  17.9 5.0 %collective-permute-start.2 = (bf16[72,242]{1,0:T(8,128)(2,1)S(1)}, bf16[72,242]{1,0:T(8,128)(2,1)S(1)}, u32[]{:S(2)}, u32[]{:S(2)}) collective-permute-start(bf16[72,242]{1,0:T(8,128)(2,1)S(1)} %get-tuple-element.539), channel_id=1, source_target_pairs={{0,6},{1,7},{2,0},{3,1},{4,2},{5,3},{6,4},{7,5},{8,14},{9,15},{10,... | collective-permute-start | bytes 104552 | tf_op jit(solution)/shard_map/ppermute | solution.py:394
  20.9 11.2 %collective-permute-start.12 = (bf16[72,912]{1,0:T(8,128)(2,1)S(1)}, bf16[72,912]{1,0:T(8,128)(2,1)S(1)}, u32[]{:S(2)}, u32[]{:S(2)}) collective-permute-start(bf16[72,912]{1,0:T(8,128)(2,1)S(1)} %pad_maximum_fusion.9), channel_id=1, source_target_pairs={{0,4},{1,5},{2,6},{3,7},{4,0},{5,1},{6,2},{7,3},{8,12},{9,13},{10,... | collective-permute-start | bytes 393992 | tf_op jit(solution)/shard_map/ppermute | solution.py:394
  22.9 7.9 %collective-permute-start.11 = (bf16[72,912]{1,0:T(8,128)(2,1)S(1)}, bf16[72,912]{1,0:T(8,128)(2,1)S(1)}, u32[]{:S(2)}, u32[]{:S(2)}) collective-permute-start(bf16[72,912]{1,0:T(8,128)(2,1)S(1)} %pad_maximum_fusion.9), channel_id=1, source_target_pairs={{0,2},{1,3},{2,4},{3,5},{4,6},{5,7},{6,0},{7,1},{8,10},{9,11},{10,... | collective-permute-start | bytes 393992 | tf_op jit(solution)/shard_map/ppermute | solution.py:394
  23.5 11.1 %collective-permute-start.13 = (bf16[72,912]{1,0:T(8,128)(2,1)S(1)}, bf16[72,912]{1,0:T(8,128)(2,1)S(1)}, u32[]{:S(2)}, u32[]{:S(2)}) collective-permute-start(bf16[72,912]{1,0:T(8,128)(2,1)S(1)} %pad_maximum_fusion.9), channel_id=1, source_target_pairs={{0,6},{1,7},{2,0},{3,1},{4,2},{5,3},{6,4},{7,5},{8,14},{9,15},{10,... | collective-permute-start | bytes 393992 | tf_op jit(solution)/shard_map/ppermute | solution.py:394
  27.3 15.7 %collective-permute-start.5 = (bf16[4,72,242]{2,1,0:T(8,128)(2,1)S(1)}, bf16[4,72,242]{2,1,0:T(8,128)(2,1)S(1)}, u32[]{:S(2)}, u32[]{:S(2)}) collective-permute-start(bf16[4,72,242]{2,1,0:T(8,128)(2,1)S(1)} %bitcast_dynamic-update-slice_fusion.20), channel_id=1, source_target_pairs={{0,24},{8,16},{16,8},{24,0},{1,25},{9,17},{17,9},{25,1},{2,26},{10... | collective-permute-start | bytes 418184 | tf_op jit(solution)/shard_map/ppermute | solution.py:403
  30.0 11.9 %collective-permute-start.4 = (bf16[4,72,242]{2,1,0:T(8,128)(2,1)S(1)}, bf16[4,72,242]{2,1,0:T(8,128)(2,1)S(1)}, u32[]{:S(2)}, u32[]{:S(2)}) collective-permute-start(bf16[4,72,242]{2,1,0:T(8,128)(2,1)S(1)} %bitcast_dynamic-update-slice_fusion.20), channel_id=1, source_target_pairs={{0,16},{8,24},{16,0},{24,8},{1,17},{9,25},{17,1},{25,9},{2,18},{10... | collective-permute-start | bytes 418184 | tf_op jit(solution)/shard_map/ppermute | solution.py:403
  30.7 7.7 %collective-permute-start.3 = (bf16[4,72,242]{2,1,0:T(8,128)(2,1)S(1)}, bf16[4,72,242]{2,1,0:T(8,128)(2,1)S(1)}, u32[]{:S(2)}, u32[]{:S(2)}) collective-permute-start(bf16[4,72,242]{2,1,0:T(8,128)(2,1)S(1)} %bitcast_dynamic-update-slice_fusion.20), channel_id=1, source_target_pairs={{0,8},{8,0},{16,24},{24,16},{1,9},{9,1},{17,25},{25,17},{2,10},{10... | collective-permute-start | bytes 418184 | tf_op jit(solution)/shard_map/ppermute | solution.py:403
  32.1 28.8 %collective-permute-start.23 = (bf16[4,192,144]{1,2,0:T(8,128)(2,1)S(1)}, bf16[4,192,144]{1,2,0:T(8,128)(2,1)S(1)}, u32[]{:S(2)}, u32[]{:S(2)}) collective-permute-start(bf16[4,192,144]{1,2,0:T(8,128)(2,1)S(1)} %bitcast_dynamic-update-slice_fusion.16), channel_id=1, source_target_pairs={{0,24},{8,16},{16,8},{24,0},{1,25},{9,17},{17,9},{25,1},{2,26},{10... | collective-permute-start | bytes 663560 | tf_op jit(solution)/shard_map/ppermute | solution.py:403
  34.6 26.3 %collective-permute-start.22 = (bf16[4,192,144]{1,2,0:T(8,128)(2,1)S(1)}, bf16[4,192,144]{1,2,0:T(8,128)(2,1)S(1)}, u32[]{:S(2)}, u32[]{:S(2)}) collective-permute-start(bf16[4,192,144]{1,2,0:T(8,128)(2,1)S(1)} %bitcast_dynamic-update-slice_fusion.16), channel_id=1, source_target_pairs={{0,16},{8,24},{16,0},{24,8},{1,17},{9,25},{17,1},{25,9},{2,18},{10... | collective-permute-start | bytes 663560 | tf_op jit(solution)/shard_map/ppermute | solution.py:403
  38.4 12.6 %collective-permute-start.21 = (bf16[4,192,144]{1,2,0:T(8,128)(2,1)S(1)}, bf16[4,192,144]{1,2,0:T(8,128)(2,1)S(1)}, u32[]{:S(2)}, u32[]{:S(2)}) collective-permute-start(bf16[4,192,144]{1,2,0:T(8,128)(2,1)S(1)} %bitcast_dynamic-update-slice_fusion.16), channel_id=1, source_target_pairs={{0,8},{8,0},{16,24},{24,16},{1,9},{9,1},{17,25},{25,17},{2,10},{10... | collective-permute-start | bytes 663560 | tf_op jit(solution)/shard_map/ppermute | solution.py:403
  41.9 32.9 %collective-permute-start.16 = (bf16[4,72,912]{2,1,0:T(8,128)(2,1)S(1)}, bf16[4,72,912]{2,1,0:T(8,128)(2,1)S(1)}, u32[]{:S(2)}, u32[]{:S(2)}) collective-permute-start(bf16[4,72,912]{2,1,0:T(8,128)(2,1)S(1)} %bitcast_dynamic-update-slice_fusion.8), channel_id=1, source_target_pairs={{0,24},{8,16},{16,8},{24,0},{1,25},{9,17},{17,9},{25,1},{2,26},{10... | collective-permute-start | bytes 1575944 | tf_op jit(solution)/shard_map/ppermute | solution.py:403
  43.0 31.0 %collective-permute-start.15 = (bf16[4,72,912]{2,1,0:T(8,128)(2,1)S(1)}, bf16[4,72,912]{2,1,0:T(8,128)(2,1)S(1)}, u32[]{:S(2)}, u32[]{:S(2)}) collective-permute-start(bf16[4,72,912]{2,1,0:T(8,128)(2,1)S(1)} %bitcast_dynamic-update-slice_fusion.8), channel_id=1, source_target_pairs={{0,16},{8,24},{16,0},{24,8},{1,17},{9,25},{17,1},{25,9},{2,18},{10... | collective-permute-start | bytes 1575944 | tf_op jit(solution)/shard_map/ppermute | solution.py:403
  51.1 22.0 %collective-permute-start.14 = (bf16[4,72,912]{2,1,0:T(8,128)(2,1)S(1)}, bf16[4,72,912]{2,1,0:T(8,128)(2,1)S(1)}, u32[]{:S(2)}, u32[]{:S(2)}) collective-permute-start(bf16[4,72,912]{2,1,0:T(8,128)(2,1)S(1)} %bitcast_dynamic-update-slice_fusion.8), channel_id=1, source_target_pairs={{0,8},{8,0},{16,24},{24,16},{1,9},{9,1},{17,25},{25,17},{2,10},{10... | collective-permute-start | bytes 1575944 | tf_op jit(solution)/shard_map/ppermute | solution.py:403
  60.8 14.9 %collective-permute-start.6 = (bf16[4,4,72,242]{3,2,1,0:T(8,128)(2,1)S(1)}, bf16[4,4,72,242]{3,2,1,0:T(8,128)(2,1)S(1)}, u32[]{:S(2)}, u32[]{:S(2)}) collective-permute-start(bf16[4,4,72,242]{3,2,1,0:T(8,128)(2,1)S(1)} %bitcast_dynamic-update-slice_fusion.12), channel_id=1, source_target_pairs={{0,1},{1,0},{2,3},{3,2},{4,5},{5,4},{6,7},{7,6},{8,9},{9,8},{10,11... | collective-permute-start | bytes 1672712 | tf_op jit(solution)/shard_map/ppermute | solution.py:398
  60.9 50.9 %collective-permute-start.24 = (bf16[4,4,192,144]{2,3,1,0:T(8,128)(2,1)S(1)}, bf16[4,4,192,144]{2,3,1,0:T(8,128)(2,1)}, u32[]{:S(2)}, u32[]{:S(2)}) collective-permute-start(bf16[4,4,192,144]{2,3,1,0:T(8,128)(2,1)S(1)} %bitcast_dynamic-update-slice_fusion.4), channel_id=1, source_target_pairs={{0,1},{1,0},{2,3},{3,2},{4,5},{5,4},{6,7},{7,6},{8,9},{9,8},{10,11... | collective-permute-start | bytes 2654216 | tf_op jit(solution)/shard_map/ppermute | solution.py:398
  75.7 72.5 %collective-permute-start.17 = (bf16[4,4,72,912]{3,2,1,0:T(8,128)(2,1)}, bf16[4,4,72,912]{3,2,1,0:T(8,128)(2,1)}, u32[]{:S(2)}, u32[]{:S(2)}) collective-permute-start(bf16[4,4,72,912]{3,2,1,0:T(8,128)(2,1)} %bitcast_dynamic-update-slice_fusion), channel_id=1, source_target_pairs={{0,1},{1,0},{2,3},{3,2},{4,5},{5,4},{6,7},{7,6},{8,9},{9,8},{10,11... | collective-permute-start | bytes 6303752 | tf_op jit(solution)/shard_map/ppermute | solution.py:398
  77.8 23.8 %copy-start.42 = (f32[576]{0:T(1024)}, f32[576]{0:T(1024)S(1)}, u32[]{:S(2)}) copy-start(f32[576]{0:T(1024)S(1)} %get-tuple-element.477) | copy-start | bytes 6916
  80.8 23.2 %collective-permute-start.8 = (bf16[272,384]{0,1:T(8,128)(2,1)}, bf16[272,384]{0,1:T(8,128)(2,1)}, u32[]{:S(2)}, u32[]{:S(2)}) collective-permute-start(bf16[272,384]{0,1:T(8,128)(2,1)} %get-tuple-element.589), channel_id=1, source_target_pairs={{0,4},{1,5},{2,6},{3,7},{8,12},{9,13},{10,14},{11,15},{16,20},{17,... | collective-permute-start | bytes 626696 | tf_op jit(solution)/shard_map/ppermute | solution.py:394
  89.2 16.0 %collective-permute-start.7 = (bf16[272,384]{0,1:T(8,128)(2,1)}, bf16[272,384]{0,1:T(8,128)(2,1)}, u32[]{:S(2)}, u32[]{:S(2)}) collective-permute-start(bf16[272,384]{0,1:T(8,128)(2,1)} %get-tuple-element.589), channel_id=1, source_target_pairs={{0,2},{1,3},{2,4},{3,5},{4,6},{5,7},{8,10},{9,11},{10,12},{11,13},... | collective-permute-start | bytes 626696 | tf_op jit(solution)/shard_map/ppermute | solution.py:394
  91.2 17.2 %collective-permute-start.9 = (bf16[272,384]{0,1:T(8,128)(2,1)}, bf16[272,384]{0,1:T(8,128)(2,1)}, u32[]{:S(2)}, u32[]{:S(2)}) collective-permute-start(bf16[272,384]{0,1:T(8,128)(2,1)} %get-tuple-element.589), channel_id=1, source_target_pairs={{0,6},{1,7},{8,14},{9,15},{16,22},{17,23},{24,30},{25,31}} | collective-permute-start | bytes 626696 | tf_op jit(solution)/shard_map/ppermute | solution.py:394
  111.7 6.7 %collective-permute-start.10 = (bf16[4,272,384]{2,1,0:T(8,128)(2,1)}, bf16[4,272,384]{2,1,0:T(8,128)(2,1)}, u32[]{:S(2)}, u32[]{:S(2)}) collective-permute-start(bf16[4,272,384]{2,1,0:T(8,128)(2,1)} %constant_dynamic-update-slice_fusion.1), channel_id=1, source_target_pairs={{0,1},{1,0},{2,3},{3,2},{4,5},{5,4},{6,7},{7,6},{8,9},{9,8},{10,11... | collective-permute-start | bytes 2506760 | tf_op jit(solution)/shard_map/ppermute | solution.py:398
  159.3 7.0 %copy-start.6 = (f32[256,576]{0,1:T(8,128)}, f32[256,576]{0,1:T(8,128)S(1)}, u32[]{:S(2)}) copy-start(f32[256,576]{0,1:T(8,128)S(1)} %get-tuple-element.602) | copy-start | bytes 1769476
  167.9 5.0 %copy-start.28 = (bf16[256,576]{0,1:T(8,128)(2,1)}, bf16[256,576]{0,1:T(8,128)(2,1)S(1)}, u32[]{:S(2)}) copy-start(bf16[256,576]{0,1:T(8,128)(2,1)S(1)} %convolution_convert_fusion.5) | copy-start | bytes 884740
  173.0 5.4 %copy-start.27 = (bf16[256,576]{0,1:T(8,128)(2,1)S(1)}, bf16[256,576]{0,1:T(8,128)(2,1)}, u32[]{:S(2)}) copy-start(bf16[256,576]{0,1:T(8,128)(2,1)} %param.31) | copy-start | bytes 884740
  212.2 51.3 %collective-permute-start.43 = (bf16[4,4,192,144]{2,3,1,0:T(8,128)(2,1)}, bf16[4,4,192,144]{2,3,1,0:T(8,128)(2,1)}, u32[]{:S(2)}, u32[]{:S(2)}) collective-permute-start(bf16[4,4,192,144]{2,3,1,0:T(8,128)(2,1)} %bitcast.391), channel_id=1, source_target_pairs={{0,1},{1,0},{2,3},{3,2},{4,5},{5,4},{6,7},{7,6},{8,9},{9,8},{10,11... | collective-permute-start | bytes 2654216 | tf_op jit(solution)/shard_map/ppermute | solution.py:398
  212.7 110.0 %collective-permute-start.36 = (bf16[4,4,72,912]{3,2,1,0:T(8,128)(2,1)}, bf16[4,4,72,912]{3,2,1,0:T(8,128)(2,1)}, u32[]{:S(2)}, u32[]{:S(2)}) collective-permute-start(bf16[4,4,72,912]{3,2,1,0:T(8,128)(2,1)} %dynamic-slice_bitcast_fusion.3), channel_id=1, source_target_pairs={{0,1},{1,0},{2,3},{3,2},{4,5},{5,4},{6,7},{7,6},{8,9},{9,8},{10,11... | collective-permute-start | bytes 6303752 | tf_op jit(solution)/shard_map/ppermute | solution.py:398
  247.0 11.0 %collective-permute-start.25 = (bf16[4,256,384]{1,2,0:T(8,128)(2,1)}, bf16[4,256,384]{1,2,0:T(8,128)(2,1)}, u32[]{:S(2)}, u32[]{:S(2)}) collective-permute-start(bf16[4,256,384]{1,2,0:T(8,128)(2,1)} %bitcast.344), channel_id=1, source_target_pairs={{0,1},{1,0},{2,3},{3,2},{4,5},{5,4},{6,7},{7,6},{8,9},{9,8},{10,11... | collective-permute-start | bytes 2359304 | tf_op jit(solution)/shard_map/ppermute | solution.py:398
  258.1 5.5 %copy-start.12 = (bf16[4,1,192,4,144]{2,1,0,4,3:T(2,128)(2,1)S(1)}, bf16[4,1,192,4,144]{2,1,0,4,3:T(2,128)(2,1)}, u32[]{:S(2)}) copy-start(bf16[4,1,192,4,144]{2,1,0,4,3:T(2,128)(2,1)} %get-tuple-element.553) | copy-start | bytes 2654212
  259.6 12.1 %collective-permute-start.26 = (bf16[256,384]{0,1:T(8,128)(2,1)S(1)}, bf16[256,384]{0,1:T(8,128)(2,1)S(1)}, u32[]{:S(2)}, u32[]{:S(2)}) collective-permute-start(bf16[256,384]{0,1:T(8,128)(2,1)S(1)} %get-tuple-element.562), channel_id=1, source_target_pairs={{2,0},{3,1},{4,2},{5,3},{6,4},{7,5},{10,8},{11,9},{12,10},{13,11},... | collective-permute-start | bytes 589832 | tf_op jit(solution)/shard_map/ppermute | solution.py:394
  260.9 19.2 %collective-permute-start.28 = (bf16[256,384]{0,1:T(8,128)(2,1)S(1)}, bf16[256,384]{0,1:T(8,128)(2,1)S(1)}, u32[]{:S(2)}, u32[]{:S(2)}) collective-permute-start(bf16[256,384]{0,1:T(8,128)(2,1)S(1)} %get-tuple-element.563), channel_id=1, source_target_pairs={{6,0},{7,1},{14,8},{15,9},{22,16},{23,17},{30,24},{31,25}} | collective-permute-start | bytes 589832 | tf_op jit(solution)/shard_map/ppermute | solution.py:394
  262.2 24.1 %collective-permute-start.27 = (bf16[256,384]{0,1:T(8,128)(2,1)S(1)}, bf16[256,384]{0,1:T(8,128)(2,1)S(1)}, u32[]{:S(2)}, u32[]{:S(2)}) collective-permute-start(bf16[256,384]{0,1:T(8,128)(2,1)S(1)} %get-tuple-element.564), channel_id=1, source_target_pairs={{4,0},{5,1},{6,2},{7,3},{12,8},{13,9},{14,10},{15,11},{20,16},{21,... | collective-permute-start | bytes 589832 | tf_op jit(solution)/shard_map/ppermute | solution.py:394
  294.7 31.8 %slice-start = ((s8[4718592]{0:T(1024)(128)(4,1)}), s8[4194304]{0:T(1024)(128)(4,1)S(1)}, s32[]{:S(2)}) async-start(s8[4718592]{0:T(1024)(128)(4,1)} %bitcast.473), calls=%async_computation | async-start | bytes 8388608
  297.2 4.7 %collective-permute-start.29 = (bf16[4,4,72,242]{3,2,1,0:T(8,128)(2,1)S(1)}, bf16[4,4,72,242]{3,2,1,0:T(8,128)(2,1)S(1)}, u32[]{:S(2)}, u32[]{:S(2)}) collective-permute-start(bf16[4,4,72,242]{3,2,1,0:T(8,128)(2,1)S(1)} %dynamic-slice_bitcast_fusion.7), channel_id=1, source_target_pairs={{0,1},{1,0},{2,3},{3,2},{4,5},{5,4},{6,7},{7,6},{8,9},{9,8},{10,11... | collective-permute-start | bytes 1672712 | tf_op jit(solution)/shard_map/ppermute | solution.py:398
  297.4 9.9 %collective-permute-start.44 = (bf16[4,192,144]{1,2,0:T(8,128)(2,1)S(1)}, bf16[4,192,144]{1,2,0:T(8,128)(2,1)S(1)}, u32[]{:S(2)}, u32[]{:S(2)}) collective-permute-start(bf16[4,192,144]{1,2,0:T(8,128)(2,1)S(1)} %get-tuple-element.565), channel_id=1, source_target_pairs={{0,8},{8,0},{16,24},{24,16},{1,9},{9,1},{17,25},{25,17},{2,10},{10... | collective-permute-start | bytes 663560 | tf_op jit(solution)/shard_map/ppermute | solution.py:403
  298.6 15.6 %collective-permute-start.46 = (bf16[4,192,144]{1,2,0:T(8,128)(2,1)S(1)}, bf16[4,192,144]{1,2,0:T(8,128)(2,1)S(1)}, u32[]{:S(2)}, u32[]{:S(2)}) collective-permute-start(bf16[4,192,144]{1,2,0:T(8,128)(2,1)S(1)} %get-tuple-element.566), channel_id=1, source_target_pairs={{0,24},{8,16},{16,8},{24,0},{1,25},{9,17},{17,9},{25,1},{2,26},{10... | collective-permute-start | bytes 663560 | tf_op jit(solution)/shard_map/ppermute | solution.py:403
  300.1 15.2 %collective-permute-start.45 = (bf16[4,192,144]{1,2,0:T(8,128)(2,1)S(1)}, bf16[4,192,144]{1,2,0:T(8,128)(2,1)S(1)}, u32[]{:S(2)}, u32[]{:S(2)}) collective-permute-start(bf16[4,192,144]{1,2,0:T(8,128)(2,1)S(1)} %get-tuple-element.567), channel_id=1, source_target_pairs={{0,16},{8,24},{16,0},{24,8},{1,17},{9,25},{17,1},{25,9},{2,18},{10... | collective-permute-start | bytes 663560 | tf_op jit(solution)/shard_map/ppermute | solution.py:403
  300.9 25.6 %slice-start.1 = ((s8[4718592]{0:T(1024)(128)(4,1)}), s8[524288]{0:T(1024)(128)(4,1)S(1)}, s32[]{:S(2)}) async-start(s8[4718592]{0:T(1024)(128)(4,1)} %bitcast.473), calls=%async_computation.1 | async-start | bytes 1048576
  302.1 14.6 %collective-permute-start.30 = (bf16[4,72,242]{2,1,0:T(8,128)(2,1)S(1)}, bf16[4,72,242]{2,1,0:T(8,128)(2,1)S(1)}, u32[]{:S(2)}, u32[]{:S(2)}) collective-permute-start(bf16[4,72,242]{2,1,0:T(8,128)(2,1)S(1)} %get-tuple-element.579), channel_id=1, source_target_pairs={{0,8},{8,0},{16,24},{24,16},{1,9},{9,1},{17,25},{25,17},{2,10},{10... | collective-permute-start | bytes 418184 | tf_op jit(solution)/shard_map/ppermute | solution.py:403
  307.2 13.1 %collective-permute-start.32 = (bf16[4,72,242]{2,1,0:T(8,128)(2,1)S(1)}, bf16[4,72,242]{2,1,0:T(8,128)(2,1)S(1)}, u32[]{:S(2)}, u32[]{:S(2)}) collective-permute-start(bf16[4,72,242]{2,1,0:T(8,128)(2,1)S(1)} %get-tuple-element.580), channel_id=1, source_target_pairs={{0,24},{8,16},{16,8},{24,0},{1,25},{9,17},{17,9},{25,1},{2,26},{10... | collective-permute-start | bytes 418184 | tf_op jit(solution)/shard_map/ppermute | solution.py:403
  314.3 8.2 %collective-permute-start.31 = (bf16[4,72,242]{2,1,0:T(8,128)(2,1)S(1)}, bf16[4,72,242]{2,1,0:T(8,128)(2,1)S(1)}, u32[]{:S(2)}, u32[]{:S(2)}) collective-permute-start(bf16[4,72,242]{2,1,0:T(8,128)(2,1)S(1)} %get-tuple-element.581), channel_id=1, source_target_pairs={{0,16},{8,24},{16,0},{24,8},{1,17},{9,25},{17,1},{25,9},{2,18},{10... | collective-permute-start | bytes 418184 | tf_op jit(solution)/shard_map/ppermute | solution.py:403
  315.5 14.8 %collective-permute-start.47 = (bf16[192,144]{0,1:T(8,128)(2,1)S(1)}, bf16[192,144]{0,1:T(8,128)(2,1)S(1)}, u32[]{:S(2)}, u32[]{:S(2)}) collective-permute-start(bf16[192,144]{0,1:T(8,128)(2,1)S(1)} %get-tuple-element.582), channel_id=1, source_target_pairs={{0,2},{1,3},{2,4},{3,5},{4,6},{5,7},{6,0},{7,1},{8,10},{9,11},{10,... | collective-permute-start | bytes 165896 | tf_op jit(solution)/shard_map/ppermute | solution.py:394
  316.8 13.6 %collective-permute-start.49 = (bf16[192,144]{0,1:T(8,128)(2,1)S(1)}, bf16[192,144]{0,1:T(8,128)(2,1)S(1)}, u32[]{:S(2)}, u32[]{:S(2)}) collective-permute-start(bf16[192,144]{0,1:T(8,128)(2,1)S(1)} %get-tuple-element.583), channel_id=1, source_target_pairs={{0,6},{1,7},{2,0},{3,1},{4,2},{5,3},{6,4},{7,5},{8,14},{9,15},{10,... | collective-permute-start | bytes 165896 | tf_op jit(solution)/shard_map/ppermute | solution.py:394
  320.3 11.6 %collective-permute-start.48 = (bf16[192,144]{0,1:T(8,128)(2,1)S(1)}, bf16[192,144]{0,1:T(8,128)(2,1)S(1)}, u32[]{:S(2)}, u32[]{:S(2)}) collective-permute-start(bf16[192,144]{0,1:T(8,128)(2,1)S(1)} %get-tuple-element.584), channel_id=1, source_target_pairs={{0,4},{1,5},{2,6},{3,7},{4,0},{5,1},{6,2},{7,3},{8,12},{9,13},{10,... | collective-permute-start | bytes 165896 | tf_op jit(solution)/shard_map/ppermute | solution.py:394
  322.6 10.0 %collective-permute-start.33 = (bf16[72,242]{1,0:T(8,128)(2,1)S(1)}, bf16[72,242]{1,0:T(8,128)(2,1)S(1)}, u32[]{:S(2)}, u32[]{:S(2)}) collective-permute-start(bf16[72,242]{1,0:T(8,128)(2,1)S(1)} %get-tuple-element.593), channel_id=1, source_target_pairs={{0,2},{1,3},{2,4},{3,5},{4,6},{5,7},{6,0},{7,1},{8,10},{9,11},{10,... | collective-permute-start | bytes 104552 | tf_op jit(solution)/shard_map/ppermute | solution.py:394
  322.7 11.9 %collective-permute-start.35 = (bf16[72,242]{1,0:T(8,128)(2,1)S(1)}, bf16[72,242]{1,0:T(8,128)(2,1)S(1)}, u32[]{:S(2)}, u32[]{:S(2)}) collective-permute-start(bf16[72,242]{1,0:T(8,128)(2,1)S(1)} %get-tuple-element.594), channel_id=1, source_target_pairs={{0,6},{1,7},{2,0},{3,1},{4,2},{5,3},{6,4},{7,5},{8,14},{9,15},{10,... | collective-permute-start | bytes 104552 | tf_op jit(solution)/shard_map/ppermute | solution.py:394
  330.3 4.9 %collective-permute-start.34 = (bf16[72,242]{1,0:T(8,128)(2,1)S(1)}, bf16[72,242]{1,0:T(8,128)(2,1)S(1)}, u32[]{:S(2)}, u32[]{:S(2)}) collective-permute-start(bf16[72,242]{1,0:T(8,128)(2,1)S(1)} %get-tuple-element.595), channel_id=1, source_target_pairs={{0,4},{1,5},{2,6},{3,7},{4,0},{5,1},{6,2},{7,3},{8,12},{9,13},{10,... | collective-permute-start | bytes 104552 | tf_op jit(solution)/shard_map/ppermute | solution.py:394
  330.3 16.6 %collective-permute-start.37 = (bf16[4,72,912]{2,1,0:T(8,128)(2,1)}, bf16[4,72,912]{2,1,0:T(8,128)(2,1)}, u32[]{:S(2)}, u32[]{:S(2)}) collective-permute-start(bf16[4,72,912]{2,1,0:T(8,128)(2,1)} %get-tuple-element.555), channel_id=1, source_target_pairs={{0,8},{8,0},{16,24},{24,16},{1,9},{9,1},{17,25},{25,17},{2,10},{10... | collective-permute-start | bytes 1575944 | tf_op jit(solution)/shard_map/ppermute | solution.py:403
  331.9 25.5 %collective-permute-start.39 = (bf16[4,72,912]{2,1,0:T(8,128)(2,1)S(1)}, bf16[4,72,912]{2,1,0:T(8,128)(2,1)}, u32[]{:S(2)}, u32[]{:S(2)}) collective-permute-start(bf16[4,72,912]{2,1,0:T(8,128)(2,1)S(1)} %get-tuple-element.556), channel_id=1, source_target_pairs={{0,24},{8,16},{16,8},{24,0},{1,25},{9,17},{17,9},{25,1},{2,26},{10... | collective-permute-start | bytes 1575944 | tf_op jit(solution)/shard_map/ppermute | solution.py:403
  332.6 25.9 %collective-permute-start.38 = (bf16[4,72,912]{2,1,0:T(8,128)(2,1)S(1)}, bf16[4,72,912]{2,1,0:T(8,128)(2,1)}, u32[]{:S(2)}, u32[]{:S(2)}) collective-permute-start(bf16[4,72,912]{2,1,0:T(8,128)(2,1)S(1)} %get-tuple-element.557), channel_id=1, source_target_pairs={{0,16},{8,24},{16,0},{24,8},{1,17},{9,25},{17,1},{25,9},{2,18},{10... | collective-permute-start | bytes 1575944 | tf_op jit(solution)/shard_map/ppermute | solution.py:403
  337.9 27.2 %copy-start.38 = (f32[72,242]{1,0:T(8,128)S(1)}, f32[72,242]{1,0:T(8,128)}, u32[]{:S(2)}) copy-start(f32[72,242]{1,0:T(8,128)} %copy-done.37) | copy-start | bytes 209092
  360.5 7.4 %collective-permute-start.40 = (bf16[72,912]{1,0:T(8,128)(2,1)S(1)}, bf16[72,912]{1,0:T(8,128)(2,1)S(1)}, u32[]{:S(2)}, u32[]{:S(2)}) collective-permute-start(bf16[72,912]{1,0:T(8,128)(2,1)S(1)} %get-tuple-element.576), channel_id=1, source_target_pairs={{0,2},{1,3},{2,4},{3,5},{4,6},{5,7},{6,0},{7,1},{8,10},{9,11},{10,... | collective-permute-start | bytes 393992 | tf_op jit(solution)/shard_map/ppermute | solution.py:394
  361.0 8.0 %collective-permute-start.42 = (bf16[72,912]{1,0:T(8,128)(2,1)S(1)}, bf16[72,912]{1,0:T(8,128)(2,1)S(1)}, u32[]{:S(2)}, u32[]{:S(2)}) collective-permute-start(bf16[72,912]{1,0:T(8,128)(2,1)S(1)} %get-tuple-element.577), channel_id=1, source_target_pairs={{0,6},{1,7},{2,0},{3,1},{4,2},{5,3},{6,4},{7,5},{8,14},{9,15},{10,... | collective-permute-start | bytes 393992 | tf_op jit(solution)/shard_map/ppermute | solution.py:394
  364.3 9.6 %collective-permute-start.41 = (bf16[72,912]{1,0:T(8,128)(2,1)S(1)}, bf16[72,912]{1,0:T(8,128)(2,1)S(1)}, u32[]{:S(2)}, u32[]{:S(2)}) collective-permute-start(bf16[72,912]{1,0:T(8,128)(2,1)S(1)} %get-tuple-element.578), channel_id=1, source_target_pairs={{0,4},{1,5},{2,6},{3,7},{4,0},{5,1},{6,2},{7,3},{8,12},{9,13},{10,... | collective-permute-start | bytes 393992 | tf_op jit(solution)/shard_map/ppermute | solution.py:394
  (39 other events, 90.8 us)
